TPU v7x, 32 devices: a whole 2x2x4 slice. The times are simulated.
32 devices in a mesh: row: 8 (over y, x, core), col: 4 (over z).
Axes of the slice: x: 2, y: 2, z: 4, core: 2. Of those that a mesh axis runs over, the one named last changes fastest.
Arguments:
- iterate: float32 [5120, 8192], P('row', 'col'), may hold values from -0.05 to 0.05
Outputs:
- update: float32 [5120, 8192], P('row', 'col')
All inputs are finite; a program needn't handle non-finite values.
Results may differ from a plain program's by a relative error of at most 0.0022.
Values may be sent and summed in bfloat16 or wider, within the bound.
No kernel may reach another device: no remote copies, remote signals or barrier semaphores. Data moves between devices by JAX's collectives and lax.ppermute only.
A program may use at most 128 MiB of HBM per device.

v0:
```python
import math

import jax
import jax.numpy as jnp
from jax import lax
from jax.sharding import PartitionSpec as P

coef_a = 3.4445
coef_b = -4.775
coef_c = 2.0315


def local(iterate):
    iter_b = iterate.astype(jnp.bfloat16)
    slab = lax.all_gather(iter_b, "row", axis=0, tiled=True)
    partial_value = lax.dot_general(
        iter_b, slab, (((1,), (1,)), ((), ())), preferred_element_type=jnp.float32
    )
    gram = lax.psum_scatter(partial_value, "col", scatter_dimension=1, tiled=True)
    gram_b = gram.astype(jnp.bfloat16)
    row_panel = lax.all_gather(gram_b, "col", axis=1, tiled=True)
    square = jnp.dot(
        row_panel,
        lax.all_gather(gram_b, "row", axis=0, tiled=True),
        preferred_element_type=jnp.float32,
    )
    mixed = (coef_b * gram + coef_c * square).astype(jnp.bfloat16)
    product = jnp.dot(
        lax.all_gather(mixed, "col", axis=1, tiled=True), slab, preferred_element_type=jnp.float32
    )
    columns_all = iterate.shape[1] * lax.axis_size("col")
    return 0.2 * math.sqrt(columns_all) * (coef_a * iterate + product)


def solution(mesh):
    return jax.shard_map(
        local,
        mesh=mesh,
        in_specs=(P("row", "col"),),
        out_specs=P("row", "col"),
        check_vma=False,
    )
```

profile of v0, /device:TPU:0, one launch (start us, length us, event | category | flops | bytes accessed | tf_op | source)
XLA Modules:
  0.0 725.7 jit_solution(11669222000012493254)
XLA Ops:
  6.5 0.0 all-gather.5.cloned.1.call-start
  6.5 4.4 convert_element_type.9
  10.9 0.0 all-gather.5.cloned.1.call-update
  10.9 0.0 reduce-scatter.2.cloned.1.call-start
  11.0 110.4 %all-gather.5.cloned.1.call-done = bf16[5120,2048]{1,0:T(8,128)(2,1)} async-done(((bf16[640,2048]{1,0:T(8,128)(2,1)}), bf16[5120,2048]{1,0:T(8,128)(2,1)}) %all-gather.5.cloned.1.call-update) | async-done | bytes 20971536 | tf_op jit(solution)/shard_map/all_gather | solution.py:15
  121.4 21.4 %fusion.2 = f32[640,5120]{1,0:T(8,128)} fusion(bf16[640,2048]{1,0:T(8,128)(2,1)} %convert_element_type.9, bf16[5120,2048]{1,0:T(8,128)(2,1)} %all-gather.5.cloned.1.call-done), kind=kOutput, calls=%fused_computation.4 | convolution fusion | flops 13421772800 | bytes 36700160 | tf_op jit(solution)/shard_map/dot_general | solution.py:16
  142.8 0.0 reduce-scatter.2.cloned.1.call-update
  142.8 0.0 all-gather.7.cloned.1.call-start
  142.8 220.4 %reduce-scatter.2.cloned.1.call-done = f32[640,1280]{1,0:T(8,128)} async-done(((f32[640,5120]{1,0:T(8,128)}), f32[640,1280]{1,0:T(8,128)}) %reduce-scatter.2.cloned.1.call-update) | async-done | bytes 3276816 | tf_op jit(solution)/shard_map/reduce_scatter | solution.py:19
  363.3 0.0 copy-start
  363.3 3.4 convert_element_type.10
  366.7 0.0 all-gather.7.cloned.1.call-update
  366.7 0.0 all-gather.9.cloned.1.call-start
  366.7 0.5 all-gather.9.cloned.1.call-update
  367.3 0.2 all-gather.11.cloned.1.call-start
  367.5 120.0 %all-gather.7.cloned.1.call-done = bf16[640,5120]{1,0:T(8,128)(2,1)} async-done(((bf16[640,1280]{1,0:T(8,128)(2,1)}), bf16[640,5120]{1,0:T(8,128)(2,1)}) %all-gather.7.cloned.1.call-update) | async-done | bytes 6553616 | tf_op jit(solution)/shard_map/all_gather | solution.py:21
  487.5 74.3 %all-gather.9.cloned.1.call-done = bf16[5120,1280]{1,0:T(8,128)(2,1)} async-done(((bf16[640,1280]{1,0:T(8,128)(2,1)}), bf16[5120,1280]{1,0:T(8,128)(2,1)}) %all-gather.9.cloned.1.call-update) | async-done | bytes 13107216 | tf_op jit(solution)/shard_map/all_gather | solution.py:24
  561.8 0.0 copy-done
  561.8 15.4 %fusion.1 = bf16[640,1280]{1,0:T(8,128)(2,1)} fusion(bf16[640,5120]{1,0:T(8,128)(2,1)} %all-gather.7.cloned.1.call-done, bf16[5120,1280]{1,0:T(8,128)(2,1)} %all-gather.9.cloned.1.call-done, f32[640,1280]{1,0:T(8,128)S(1)} %copy-done), kind=kOutput, calls=%fused_computation.3 | convolution fusion | flops 8391884800 | bytes 24576000 | tf_op jit(solution)/shard_map/dot_general | solution.py:22
  577.3 0.0 all-gather.11.cloned.1.call-update
  577.3 119.8 %all-gather.11.cloned.1.call-done = bf16[640,5120]{1,0:T(8,128)(2,1)} async-done(((bf16[640,1280]{1,0:T(8,128)(2,1)}), bf16[640,5120]{1,0:T(8,128)(2,1)}) %all-gather.11.cloned.1.call-update) | async-done | bytes 6553616 | tf_op jit(solution)/shard_map/all_gather | solution.py:29
  697.1 22.1 %add_multiply_fusion = f32[640,2048]{1,0:T(8,128)} fusion(f32[640,2048]{1,0:T(8,128)} %param.1, bf16[640,5120]{1,0:T(8,128)(2,1)} %all-gather.11.cloned.1.call-done, bf16[5120,2048]{1,0:T(8,128)(2,1)} %all-gather.5.cloned.1.call-done), kind=kOutput, calls=%fused_computation | convolution fusion | flops 13425704960 | bytes 38010880 | tf_op jit(solution)/shard_map/dot_general | solution.py:28
Async XLA Ops:
  6.5 114.9 %all-gather.5.cloned.1.call-start = ((), (), s32[]{:S(2)}) async-start(), calls=%async_computation.1 | async-start | bytes 23592960 | tf_op jit(solution)/shard_map/all_gather | solution.py:15
  10.9 352.3 %reduce-scatter.2.cloned.1.call-start = ((), (), s32[]{:S(2)}) async-start(), calls=%async_computation.2 | async-start | bytes 16384000 | tf_op jit(solution)/shard_map/reduce_scatter | solution.py:19
  142.8 344.7 %all-gather.7.cloned.1.call-start = ((), (), s32[]{:S(2)}) async-start(), calls=%async_computation.3 | async-start | bytes 8192000 | tf_op jit(solution)/shard_map/all_gather | solution.py:21
  363.3 198.6 %copy-start = (f32[640,1280]{1,0:T(8,128)S(1)}, f32[640,1280]{1,0:T(8,128)}, u32[]{:S(2)}) copy-start(f32[640,1280]{1,0:T(8,128)} %reduce-scatter.2.cloned.1.call-done) | copy-start | bytes 9830404
  366.7 195.2 %all-gather.9.cloned.1.call-start = ((), (), s32[]{:S(2)}) async-start(), calls=%async_computation.4 | async-start | bytes 14745600 | tf_op jit(solution)/shard_map/all_gather | solution.py:24
  367.3 329.8 %all-gather.11.cloned.1.call-start = ((), (), s32[]{:S(2)}) async-start(), calls=%async_computation.5 | async-start | bytes 8192000 | tf_op jit(solution)/shard_map/all_gather | solution.py:29
Sparse Core Ops, SparseCore 0:
  11.1 110.2 all-gather.4
  142.9 220.2 reduce-scatter.1
  366.8 120.6 all-gather.6
  489.3 72.5 all-gather.8
  577.4 119.6 all-gather.10
where the time goes:
time: 726 us
  waiting for transfers between devices  646 us (89%)
  matrix products  58.9 us (8%)
  between operations  13.1 us (2%)
  other arithmetic  7.78 us (1%)
    reduce_scatter x1, waiting for transfers between devices, local(): lax.psum_scatter(partial_value, 'col', scatter_dimension=1, tiled=True)  220 us
    all_gather x1, waiting for transfers between devices, local(): row_panel = lax.all_gather(gram_b, 'col', axis=1, tiled=True)  120 us
    all_gather x1, waiting for transfers between devices, local(): lax.all_gather(mixed, 'col', axis=1, tiled=True)  120 us
    all_gather x1, waiting for transfers between devices, local(): slab = lax.all_gather(iter_b, 'row', axis=0, tiled=True)  110 us
    all_gather x1, waiting for transfers between devices, local(): lax.all_gather(gram_b, 'row', axis=0, tiled=True)  74.3 us
    dot_general x1, matrix products, local(): jnp.dot(lax.all_gather(mixed, 'col', axis=1, tiled=True), slab, preferred...  22.1 us
    dot_general x1, matrix products, local(): lax.dot_general(iter_b, slab, (((1,), (1,)), ((), ())), preferred_element...  21.4 us
    dot_general x1, matrix products, local(): jnp.dot(row_panel, lax.all_gather(gram_b, 'row', axis=0, tiled=True), pre...  15.4 us
  transfers between devices with their start and end apart: 5, of which 5 were waited for; matrix products, arithmetic and copies ran while one was open for 0% of the time, Pallas kernels for 0%

commit v1 on v0

--- a/solution.py
+++ b/solution.py
@@ -2,15 +2,21 @@
 
 import jax
 import jax.numpy as jnp
+import numpy as np
 from jax import lax
+from jax.experimental import pallas as pl
+from jax.experimental.pallas import tpu as pltpu
 from jax.sharding import PartitionSpec as P
 
 coef_a = 3.4445
 coef_b = -4.775
 coef_c = 2.0315
 
-
-def local(iterate):
+SCALE_X = 32.0
+SCALE_G = SCALE_X * SCALE_X
+
+
+def plain(iterate):
     iter_b = iterate.astype(jnp.bfloat16)
     slab = lax.all_gather(iter_b, "row", axis=0, tiled=True)
     partial_value = lax.dot_general(
@@ -32,9 +38,331 @@
     return 0.2 * math.sqrt(columns_all) * (coef_a * iterate + product)
 
 
+def partner(r, d):
+    c, k = r // 2, r % 2
+    high = c & 1 if d == 1 else (c >> 1) & 1
+    return 2 * (c ^ d) + (k ^ high)
+
+
+def giver(r, d):
+    return next(q for q in range(8) if partner(q, d) == r)
+
+
+def on_chip(r, c):
+    return r // 2 == c
+
+
+FETCH = {d: [(partner(r, d), r) for r in range(8)] for d in (1, 2, 3)}
+GIVE = {d: [(q, partner(q, d)) for q in range(8)] for d in (1, 2, 3)}
+SIBLING = [(r, r ^ 1) for r in range(8)]
+
+
+def forward(via, held, wanted):
+    pairs = []
+    for r in range(8):
+        s = [s for s in range(8) if on_chip(s, (r // 2) ^ via) and held(s) == wanted(r)]
+        pairs.append((s[0], r))
+    return pairs
+
+
+FETCH_X = forward(1, lambda s: partner(s, 2), lambda r: partner(r, 3))
+FETCH_Y = forward(2, lambda s: partner(s, 1), lambda r: partner(r, 3))
+GIVE_X = forward(1, lambda s: giver(s, 2), lambda r: giver(r, 3))
+GIVE_Y = forward(2, lambda s: giver(s, 1), lambda r: giver(r, 3))
+
+
+def device_order(r):
+    order = [r, r ^ 1]
+    for d in (1, 2, 3):
+        order += [partner(r, d), partner(r, d) ^ 1]
+    return order
+
+
+def tables():
+    groups = {"de": [], 1: [], 2: [], 3: []}
+    for r in range(8):
+        order = device_order(r)
+        slot = {q: i for i, q in enumerate(order)}
+        de = [(i, i) for i in range(8)]
+        for i in range(0, 8, 2):
+            c = order[i] // 2
+            de.append((slot[2 * c], slot[2 * c + 1]))
+        groups["de"].append(de)
+        for d in (1, 2, 3):
+            assert order[2 * d + 1] == giver(r, d)
+            groups[d].append([(i, slot[partner(order[i], d)]) for i in range(8)])
+    return {g: np.asarray(t, np.int32) for g, t in groups.items()}
+
+
+TABLES = tables()
+
+
+def nt(a, b):
+    return lax.dot_general(a, b, (((1,), (1,)), ((), ())), preferred_element_type=jnp.float32)
+
+
+def square_kernel(*refs, items, sources, first, last):
+    table, panel = refs[0], refs[1]
+    inputs = refs[2 : 2 + sources]
+    rest = refs[2 + sources :]
+    if not first:
+        before, rest = rest[0], rest[1:]
+    if last:
+        low, rest = rest[0], rest[1:]
+        out, slots, sems, total = rest
+    else:
+        total, slots, sems = rest
+    size = panel.shape[0]
+    half = size // 2
+
+    def copies(n):
+        slot = n % 2
+        parts = items[n]
+        if len(parts) == 1:
+            m, at = parts[0]
+            return [(None, inputs[m].at[pl.ds(at, size)], slots.at[slot], sems.at[slot])]
+        (m, at), (p, to) = parts
+        top, bottom = slots.at[slot, pl.ds(0, half)], slots.at[slot, pl.ds(half, size - half)]
+        one, two = inputs[m].at[pl.ds(at, half)], inputs[p].at[pl.ds(to, half)]
+        return [(True, one, top, sems.at[slot]), (True, two, bottom, sems.at[slot]),
+                (False, two, top, sems.at[slot]), (False, one, bottom, sems.at[slot])]
+
+    def start(n):
+        straight = table[3 * n + 2] == 1
+        for when, src, dst, sem in copies(n):
+            if when is None:
+                pltpu.make_async_copy(src, dst, sem).start()
+            else:
+                @pl.when(straight == when)
+                def _():
+                    pltpu.make_async_copy(src, dst, sem).start()
+
+    start(0)
+    if first:
+        total[...] = jnp.zeros_like(total)
+    else:
+        total[...] = before[...]
+
+    def body(n, carry):
+        for k in range(1, len(items)):
+            @pl.when(n + 1 == k)
+            def _():
+                start(k)
+
+        slot = n % 2
+        pltpu.make_async_copy(slots.at[1 - slot], slots.at[slot], sems.at[slot]).wait()
+        i, j = table[3 * n], table[3 * n + 1]
+        rows = pl.ds(pl.multiple_of(i * size, 128), size)
+        cols = pl.ds(pl.multiple_of(j * size, 128), size)
+        block = slots[slot]
+        total[:, cols] += jnp.dot(panel[:, rows], block, preferred_element_type=jnp.float32)
+
+        @pl.when(i != j)
+        def _():
+            total[:, rows] += nt(panel[:, cols], block)
+
+        return carry
+
+    lax.fori_loop(0, len(items), body, 0)
+    if last:
+        for k in range(8):
+            at = pl.ds(k * size, size)
+            gram = panel[:, at].astype(jnp.float32) + low[:, at].astype(jnp.float32)
+            out[:, at] = (
+                (coef_b / SCALE_G) * gram + (coef_c / SCALE_G**2) * total[:, at]
+            ).astype(out.dtype)
+
+
+def square_update(rows, items, inputs, panel, before=None, low=None):
+    size, wide = panel.shape
+    first, last = before is None, low is not None
+    vmem = pl.BlockSpec(memory_space=pltpu.VMEM)
+    operands = [rows.reshape(-1), panel, *inputs]
+    specs = [pl.BlockSpec(memory_space=pltpu.SMEM), vmem] + [pl.BlockSpec(memory_space=pl.ANY)] * len(inputs)
+    if not first:
+        operands.append(before)
+        specs.append(vmem)
+    if last:
+        operands.append(low)
+        specs.append(vmem)
+    scratch = [pltpu.VMEM((2, size, size), jnp.bfloat16), pltpu.SemaphoreType.DMA((2,))]
+    if last:
+        scratch.append(pltpu.VMEM((size, wide), jnp.float32))
+    n = len(items)
+    return pl.pallas_call(
+        lambda *refs: square_kernel(
+            *refs, items=items, sources=len(inputs), first=first, last=last
+        ),
+        in_specs=specs,
+        out_specs=vmem,
+        out_shape=jax.ShapeDtypeStruct((size, wide), jnp.bfloat16 if last else jnp.float32),
+        scratch_shapes=scratch,
+        compiler_params=pltpu.CompilerParams(vmem_limit_bytes=56 * 2**20),
+        cost_estimate=pl.CostEstimate(
+            flops=4 * n * size**3,
+            bytes_accessed=2 * n * size * size + 10 * size * wide,
+            transcendentals=0,
+        ),
+    )(*operands)
+
+
+def last_kernel(mixed, x, *refs, scale):
+    slab, out = refs[:-1], refs[-1]
+    size = mixed.shape[0]
+    total = jnp.dot(mixed[:, :size], slab[0][...], preferred_element_type=jnp.float32)
+    for k in range(1, 8):
+        total += jnp.dot(
+            mixed[:, k * size : (k + 1) * size], slab[k][...], preferred_element_type=jnp.float32
+        )
+    out[...] = (scale * coef_a) * x[...] + (scale / SCALE_X) * total
+
+
+def last_product(mixed, x, slab, scale):
+    size, width = x.shape
+    tile = 512
+    column = pl.BlockSpec((size, tile), lambda s: (0, s))
+    return pl.pallas_call(
+        lambda *refs: last_kernel(*refs, scale=scale),
+        grid=(width // tile,),
+        in_specs=[pl.BlockSpec(mixed.shape, lambda s: (0, 0), pipeline_mode=pl.Buffered(1))]
+        + [column] * 9,
+        out_specs=column,
+        out_shape=jax.ShapeDtypeStruct(x.shape, jnp.float32),
+        compiler_params=pltpu.CompilerParams(vmem_limit_bytes=52 * 2**20),
+        cost_estimate=pl.CostEstimate(
+            flops=16 * size * size * width, bytes_accessed=24 * size * width, transcendentals=0
+        ),
+    )(mixed, x, *slab)
+
+
+def to_half(x):
+    return lax.reduce_precision(x, 5, 10).astype(jnp.float16)
+
+
+def encode(x):
+    near = lax.reduce_precision(x, 5, 10)
+    goal = lax.reduce_precision(x, 8, 7)
+    same = lax.reduce_precision(near, 8, 7) == goal
+    return jnp.where(same, near, near + 0.25 * (goal - near)).astype(jnp.float16)
+
+
+def plane_sum(part, inner, fix=lambda x: x):
+    got = lax.ppermute(to_half(part), "col", [(0, 1), (3, 2)])
+    pair = part + got.astype(jnp.float32)
+    got = lax.ppermute(to_half(pair), "col", [(1, 2), (2, 1)])
+    mine = encode(fix(pair + got.astype(jnp.float32)))
+    return jnp.where(inner, mine, lax.ppermute(mine, "col", [(1, 0), (2, 3)]))
+
+
+def send(x, pairs):
+    return lax.ppermute(x, "row", pairs)
+
+
+def gather_slab(x):
+    half = x.shape[0] // 2
+    one, two = send(x, FETCH[1]), send(x, FETCH[2])
+    three = jnp.concatenate([send(two[:half], FETCH_X), send(one[half:], FETCH_Y)])
+    return one, two, three
+
+
+def gather_unit(u):
+    half = u.shape[0] // 2
+    one, two = send(u, GIVE[1]), send(u, GIVE[2])
+    three = jnp.concatenate([send(two[:half], GIVE_X), send(one[half:], GIVE_Y)])
+    out = [u, send(u, SIBLING)]
+    for m in (one, two, three):
+        out += [send(m, SIBLING), m]
+    return out
+
+
+def local(iterate):
+    size, width = iterate.shape
+    half = size // 2
+    me = lax.axis_index("row")
+    core = me % 2
+    plane = lax.axis_index("col")
+    inner = (plane == 1) | (plane == 2)
+    table = {g: jnp.asarray(t)[me] for g, t in TABLES.items()}
+
+    x = (iterate * SCALE_X).astype(jnp.bfloat16)
+    sib = send(x, SIBLING)
+    one, two, three = gather_slab(x)
+
+    xf = x.astype(jnp.float32)
+    diag = lax.psum(jnp.sum(xf * xf, axis=1), "col")
+    eye = lax.broadcasted_iota(jnp.int32, (size, size), 0) == lax.broadcasted_iota(
+        jnp.int32, (size, size), 1
+    )
+    d_part = nt(x, x)
+    e_part = nt(
+        jnp.where(core == 0, x[:half], sib[half:]), jnp.where(core == 0, sib, x)
+    )
+    put_diag = lambda t: jnp.concatenate([jnp.where(eye, diag[:, None], t[:size]), t[size:]])
+    unit_de = plane_sum(jnp.concatenate([d_part, e_part]), inner, put_diag)
+    unit = {d: plane_sum(nt(x, v), inner) for d, v in ((1, one), (2, two), (3, three))}
+
+    all_de = gather_unit(unit_de)
+    every = {d: gather_unit(unit[d]) for d in (1, 2, 3)}
+    slab = [x, sib]
+    for v in (one, two, three):
+        slab += [v, send(v, SIBLING)]
+
+    de = [m.astype(jnp.bfloat16) for m in all_de]
+    e_rows = jnp.where(
+        core == 0,
+        jnp.concatenate([all_de[0][size:], all_de[1][size:]]),
+        jnp.concatenate([all_de[1][size:], all_de[0][size:]]),
+    )
+    panel = [unit_de[:size], jnp.where(core == 0, e_rows, e_rows.T)]
+    for d in (1, 2, 3):
+        panel += [unit[d], every[d][2 * d + 1].T]
+    panel = jnp.concatenate(panel, axis=1)
+    panel_b = panel.astype(jnp.bfloat16)
+    whole = panel.astype(jnp.float32)
+    goal = lax.reduce_precision(whole, 8, 7)
+    diag_low = jnp.where(eye, diag[:, None], whole[:, :size])
+    low = jnp.concatenate([diag_low, whole[:, size:]], axis=1)
+    low = (low - goal).astype(jnp.bfloat16)
+
+    f = {d: [m.astype(jnp.bfloat16) for m in every[d]] for d in (1, 2, 3)}
+
+    def update(wanted, before=None, low=None):
+        inputs, items, rows = [], [], []
+
+        def place(m):
+            for k, known in enumerate(inputs):
+                if known is m:
+                    return k
+            inputs.append(m)
+            return len(inputs) - 1
+
+        for kind, k in wanted:
+            if kind == "d":
+                items.append([(place(de[k]), 0)])
+                rows.append(jnp.array([k, k, 1], jnp.int32))
+            elif kind == "e":
+                items.append([(place(de[k]), size), (place(de[k + 1]), size)])
+                at = table["de"][8 + k // 2]
+                rows.append(jnp.concatenate([at, (at[:1] == k).astype(jnp.int32)]))
+            else:
+                items.append([(place(f[kind][k]), 0)])
+                rows.append(jnp.concatenate([table[kind][k], jnp.ones(1, jnp.int32)]))
+        return square_update(jnp.stack(rows), items, inputs, panel_b, before, low)
+
+    total = update(
+        [("d", k) for k in range(8)]
+        + [("e", k) for k in range(0, 8, 2)]
+        + [(d, k) for d in (1, 2) for k in range(8)]
+    )
+    mixed = update([(3, k) for k in range(8)], total, low)
+    scale = 0.2 * math.sqrt(width * lax.axis_size("col"))
+    return last_product(mixed, iterate, slab, scale)
+
+
 def solution(mesh):
+    suits = mesh.shape["row"] == 8 and mesh.shape["col"] == 4
     return jax.shard_map(
-        local,
+        local if suits else plain,
         mesh=mesh,
         in_specs=(P("row", "col"),),
         out_specs=P("row", "col"),

time: 726 us -> 610 us (0.84); the launches traced: 726 us -> 599 us
  waiting for transfers between devices: 646 us -> 138 us
  other arithmetic: 7.78 us -> 118 us
  Pallas kernels: 0 us -> 109 us
  local copies, waits for them, and re-layouts: 0.01 us -> 105 us
  starting transfers between devices: 0.35 us -> 53.5 us
  blocking collectives: 0 us -> 45.3 us
  matrix products: 58.9 us -> 27.5 us
  between operations: 13.1 us -> 3.63 us
    all_gather x4 -> x0, waiting for transfers between devices: 425 us -> none  [the longest x1 120 us: local(): row_panel = lax.all_gather(gram_b, 'col', axis=1, tiled=True)]
    reduce_scatter x1 -> x0, waiting for transfers between devices: 220 us -> none  [local(): lax.psum_scatter(partial_value, 'col', scatter_dimension=1, tiled=True)]
    ppermute x0 -> x52, waiting for transfers between devices: none -> 138 us  [the longest x40 101 us: send(): return lax.ppermute(x, 'row', pairs)]
    pallas_call x0 -> x3, Pallas kernels: none -> 109 us  [the longest x2 84.4 us: square_update(): pl.pallas_call(lambda *refs: square_kernel(*refs, items=items, sources=le...]
    convert_element_type x2 -> x43, other arithmetic: 7.78 us -> 104 us  [the longest x24 42.4 us: local(): f = {d: [m.astype(jnp.bfloat16) for m in every[d]] for d in (1, 2, 3)}]
    ppermute x0 -> x52, starting transfers between devices: none -> 53.5 us  [the longest x40 28.8 us: send(): return lax.ppermute(x, 'row', pairs)]
    convert_element_type x0 -> x24, local copies, waits for them, and re-layouts: none -> 48.5 us  [local(): f = {d: [m.astype(jnp.bfloat16) for m in every[d]] for d in (1, 2, 3)}]
    psum x0 -> x1, blocking collectives: none -> 45.3 us  [local(): diag = lax.psum(jnp.sum(xf * xf, axis=1), 'col')]
  transfers between devices with their start and end apart: 5 -> 52, of which waited for: 5 -> 9; matrix products, arithmetic and copies ran while one was open for 0% -> 40% of each run, Pallas kernels for 0% -> 14%
where the time goes in v1:
time: 610 us; the launch traced here: 599 us
  waiting for transfers between devices  138 us (23%)
  other arithmetic  118 us (19%)
  Pallas kernels  109 us (18%)
  local copies, waits for them, and re-layouts  105 us (17%)
  starting transfers between devices  53.5 us (9%)
  blocking collectives  45.3 us (7%)
  matrix products  27.5 us (5%)
    ppermute x40, waiting for transfers between devices, send(): return lax.ppermute(x, 'row', pairs)  101 us
    pallas_call x2, Pallas kernels, square_update(): pl.pallas_call(lambda *refs: square_kernel(*refs, items=items, sources=le...  84.4 us
    convert_element_type x24, local copies, waits for them, and re-layouts, local(): f = {d: [m.astype(jnp.bfloat16) for m in every[d]] for d in (1, 2, 3)}  48.5 us
    psum x1, blocking collectives, local(): diag = lax.psum(jnp.sum(xf * xf, axis=1), 'col')  45.3 us
    convert_element_type x24, other arithmetic, local(): f = {d: [m.astype(jnp.bfloat16) for m in every[d]] for d in (1, 2, 3)}  42.4 us
    ppermute x4, waiting for transfers between devices, plane_sum(): return jnp.where(inner, mine, lax.ppermute(mine, 'col', [(1, 0), (2, 3)]))  29.8 us
    ppermute x40, starting transfers between devices, send(): return lax.ppermute(x, 'row', pairs)  28.8 us
    dot_general x5, matrix products, nt(): lax.dot_general(a, b, (((1,), (1,)), ((), ())), preferred_element_type=jn...  27.5 us
  transfers between devices with their start and end apart: 52, of which 9 were waited for; matrix products, arithmetic and copies ran while one was open for 40% of the time, Pallas kernels for 14%

profile of v1, /device:TPU:0, one launch (start us, length us, event | category | flops | bytes accessed | tf_op | source)
XLA Modules:
  0.0 598.8 jit_solution(4244422649578220337)
XLA Ops:
  0.0 4.6 multiply_reduce_fusion
  9.5 4.9 fusion.47
  14.4 50.4 %collective-permute-done.10.refs_6_ = bf16[640,2048]{1,0:T(8,128)(2,1)} collective-permute-done((bf16[640,2048]{1,0:T(8,128)(2,1)}, bf16[640,2048]{1,0:T(8,128)(2,1)}, u32[]{:S(2)}, u32[]{:S(2)}) %collective-permute-start.10) | collective-permute-done | bytes 2621472 | tf_op jit(solution)/shard_map/ppermute | solution.py:258
  69.0 3.8 fusion.1
  75.2 4.6 collective-permute-start.1
  79.8 6.7 %reduce-precision_convert_fusion.7 = (f16[640,640]{0,1:T(8,128)(2,1)}, f32[640,640]{0,1:T(8,128)}) fusion(bf16[640,2048]{1,0:T(8,128)(2,1)} %get-tuple-element.20.refs_2_, bf16[640,2048]{1,0:T(8,128)(2,1)} %collective-permute-done.5.refs_4_), kind=kOutput, calls=%fused_computation.35 | convolution fusion | flops 1678540800 | bytes 7700480 | tf_op jit(solution)/shard_map/dot_general | solution.py:101
  87.8 6.7 %reduce-precision_convert_fusion.5 = (f16[640,640]{0,1:T(8,128)(2,1)}, f32[640,640]{0,1:T(8,128)}) fusion(bf16[640,2048]{1,0:T(8,128)(2,1)} %get-tuple-element.20.refs_2_, bf16[640,2048]{1,0:T(8,128)(2,1)} %collective-permute-done.10.refs_6_), kind=kOutput, calls=%fused_computation.31 | convolution fusion | flops 1678540800 | bytes 7700480 | tf_op jit(solution)/shard_map/dot_general | solution.py:101
  100.7 45.3 %psum.7 = f32[640]{0:T(1024)S(1)} all-reduce(f32[640]{0:T(1024)S(1)} %get-tuple-element.19), channel_id=1, replica_groups=mesh['row'=8,'col'=4] {'col'}, use_global_device_ids=true, to_apply=%region_1.2 | all-reduce | flops 640 | bytes 5120 | tf_op jit(solution)/shard_map/psum | solution.py:292
  159.2 5.4 reduce-precision_convert_fusion.3
  164.7 8.3 %collective-permute-start.17 = (f16[640,640]{0,1:T(8,128)(2,1)S(1)}, f16[640,640]{0,1:T(8,128)(2,1)S(1)}, u32[]{:S(2)}, u32[]{:S(2)}) collective-permute-start(f16[640,640]{0,1:T(8,128)(2,1)S(1)} %get-tuple-element.59), channel_id=1, source_target_pairs={{0,1},{3,2},{4,5},{7,6},{8,9},{11,10},{12,13},{15,14},{16,17},{19,... | collective-permute-start | bytes 2457608 | tf_op jit(solution)/shard_map/ppermute | solution.py:250
  180.4 7.1 %collective-permute-done.17 = f16[640,640]{0,1:T(8,128)(2,1)S(1)} collective-permute-done((f16[640,640]{0,1:T(8,128)(2,1)S(1)}, f16[640,640]{0,1:T(8,128)(2,1)S(1)}, u32[]{:S(2)}, u32[]{:S(2)}) %collective-permute-start.17) | collective-permute-done | bytes 819232 | tf_op jit(solution)/shard_map/ppermute | solution.py:250
  189.2 24.3 %collective-permute-done.13 = f16[640,640]{0,1:T(8,128)(2,1)S(1)} collective-permute-done((f16[640,640]{0,1:T(8,128)(2,1)S(1)}, f16[640,640]{0,1:T(8,128)(2,1)S(1)}, u32[]{:S(2)}, u32[]{:S(2)}) %collective-permute-start.13) | collective-permute-done | bytes 819232 | tf_op jit(solution)/shard_map/ppermute | solution.py:254
  217.7 5.5 collective-permute-done.8
  224.9 3.9 collective-permute-start.37
  235.6 18.7 %collective-permute-done.9 = f16[640,640]{0,1:T(8,128)(2,1)S(1)} collective-permute-done((f16[640,640]{0,1:T(8,128)(2,1)S(1)}, f16[640,640]{0,1:T(8,128)(2,1)S(1)}, u32[]{:S(2)}, u32[]{:S(2)}) %collective-permute-start.9) | collective-permute-done | bytes 819232 | tf_op jit(solution)/shard_map/ppermute | solution.py:258
  258.7 9.2 %collective-permute-done.46 = f16[320,640]{0,1:T(8,128)(2,1)S(1)} collective-permute-done((f16[320,640]{0,1:T(8,128)(2,1)S(1)}, f16[320,640]{0,1:T(8,128)(2,1)S(1)}, u32[]{:S(2)}, u32[]{:S(2)}) %collective-permute-start.46) | collective-permute-done | bytes 409632 | tf_op jit(solution)/shard_map/ppermute | solution.py:258
  272.4 8.4 %collective-permute-done.40 = f16[320,640]{0,1:T(8,128)(2,1)S(1)} collective-permute-done((f16[320,640]{0,1:T(8,128)(2,1)S(1)}, f16[320,640]{0,1:T(8,128)(2,1)S(1)}, u32[]{:S(2)}, u32[]{:S(2)}) %collective-permute-start.40) | collective-permute-done | bytes 409632 | tf_op jit(solution)/shard_map/ppermute | solution.py:258
  297.1 12.5 %collective-permute-done.20 = f16[640,640]{0,1:T(8,128)(2,1)} collective-permute-done((f16[640,640]{0,1:T(8,128)(2,1)}, f16[640,640]{0,1:T(8,128)(2,1)}, u32[]{:S(2)}, u32[]{:S(2)}) %collective-permute-start.20) | collective-permute-done | bytes 819232 | tf_op jit(solution)/shard_map/ppermute | solution.py:258
  431.3 14.9 %fusion.46 = (f32[640,5120]{1,0:T(8,128)}, bf16[640,5120]{1,0:T(8,128)(2,1)}) fusion(f16[640,5120]{1,0:T(8,128)(2,1)} %bitcast_dynamic-update-slice_fusion), kind=kLoop, calls=%fused_computation.159 | loop fusion | flops 6553600 | bytes 26214400 | tf_op jit(solution)/shard_map/convert_element_type | solution.py:321
  446.2 9.2 %slice.260 = f32[640,4480]{1,0:T(8,128)} slice(f32[640,5120]{1,0:T(8,128)} %get-tuple-element.21), slice={[0:640], [640:5120]} | slice | bytes 22937600 | tf_op jit(solution)/shard_map/slice | solution.py:324
  460.8 10.0 %fusion.refs_11_ = bf16[640,5120]{1,0:T(8,128)(2,1)} fusion(f32[640,4480]{1,0:T(8,128)} %slice.260, f32[640,640]{1,0:T(8,128)S(1)} %slice_select_fusion, f16[640,5120]{1,0:T(8,128)(2,1)} %bitcast_dynamic-update-slice_fusion), kind=kLoop, calls=%fused_computation.1 | loop fusion | flops 16384000 | bytes 26214400 | tf_op jit(solution)/shard_map/convert_element_type | solution.py:325
  488.2 54.4 %shard_map.127.refs_10_ = f32[640,5120]{1,0:T(8,128)} custom-call(s32[84]{0:T(128)} %reshape.84.refs_0_, bf16[640,5120]{1,0:T(8,128)(2,1)} %get-tuple-element.22.refs_1_, bf16[960,640]{1,0:T(8,128)(2,1)} %get-tuple-element.13.refs_2_, bf16[960,640]{1,0:T(8,128)(2,1)} %convert_element_type.235.refs_3_, bf16[960,640]{1,0:T(8,128)(2,1)} %convert_element_type.236.refs_4_, ...), custom_call_target="tpu_custom_call" | custom-call | flops 29360128000 | bytes 55705600 | tf_op jit(solution)/shard_map/pallas_call | solution.py:192
  542.6 30.0 %shard_map.128.refs_0_ = bf16[640,5120]{1,0:T(8,128)(2,1)} custom-call(s32[24]{0:T(128)} %reshape.83.refs_0_, bf16[640,5120]{1,0:T(8,128)(2,1)} %get-tuple-element.22.refs_1_, bf16[640,640]{1,0:T(8,128)(2,1)} %copy.139.refs_2_, bf16[640,640]{1,0:T(8,128)(2,1)} %copy.140.refs_3_, bf16[640,640]{1,0:T(8,128)(2,1)} %copy.141.refs_4_, ...), custom_call_target="tpu_custom_call" | custom-call | flops 8388608000 | bytes 39321600 | tf_op jit(solution)/shard_map/pallas_call | solution.py:192
  574.1 24.2 %shard_map.129 = f32[640,2048]{1,0:T(8,128)} custom-call(bf16[640,5120]{1,0:T(8,128)(2,1)} %shard_map.128.refs_0_, f32[640,2048]{1,0:T(8,128)} %refs_1_.1, bf16[640,2048]{1,0:T(8,128)(2,1)} %get-tuple-element.20.refs_2_, bf16[640,2048]{1,0:T(8,128)(2,1)} %collective-permute-done.refs_3_, bf16[640,2048]{1,0:T(8,128)(2,1)} %collective-permute-done.5.refs_4_, ...), custom_call_target="tpu_custom_call" | custom-call | flops 13421772800 | bytes 31457280 | tf_op jit(solution)/shard_map/pallas_call | solution.py:224
  (270 shorter events, 222.3 us)
Async XLA Ops:
  4.6 60.1 %collective-permute-start.10 = (bf16[640,2048]{1,0:T(8,128)(2,1)}, bf16[640,2048]{1,0:T(8,128)(2,1)}, u32[]{:S(2)}, u32[]{:S(2)}) collective-permute-start(bf16[640,2048]{1,0:T(8,128)(2,1)} %get-tuple-element.20.refs_2_), channel_id=1, source_target_pairs={{16,0},{20,4},{24,8},{28,12},{4,16},{0,20},{12,24},{8,28},{17,1},{... | collective-permute-start | bytes 7864328 | tf_op jit(solution)/shard_map/ppermute | solution.py:258
  7.0 62.0 %collective-permute-start = (bf16[640,2048]{1,0:T(8,128)(2,1)}, bf16[640,2048]{1,0:T(8,128)(2,1)}, u32[]{:S(2)}, u32[]{:S(2)}) collective-permute-start(bf16[640,2048]{1,0:T(8,128)(2,1)} %get-tuple-element.20.refs_2_), channel_id=1, source_target_pairs={{0,4},{4,0},{8,12},{12,8},{16,20},{20,16},{24,28},{28,24},{1,5},{5... | collective-permute-start | bytes 7864328 | tf_op jit(solution)/shard_map/ppermute | solution.py:258
  7.7 72.1 %collective-permute-start.5 = (bf16[640,2048]{1,0:T(8,128)(2,1)}, bf16[640,2048]{1,0:T(8,128)(2,1)}, u32[]{:S(2)}, u32[]{:S(2)}) collective-permute-start(bf16[640,2048]{1,0:T(8,128)(2,1)} %get-tuple-element.20.refs_2_), channel_id=1, source_target_pairs={{8,0},{12,4},{4,8},{0,12},{24,16},{28,20},{20,24},{16,28},{9,1},{1... | collective-permute-start | bytes 7864328 | tf_op jit(solution)/shard_map/ppermute | solution.py:258
  67.3 89.1 %collective-permute-start.15 = (bf16[320,2048]{1,0:T(8,128)(2,1)}, bf16[320,2048]{1,0:T(8,128)(2,1)}, u32[]{:S(2)}, u32[]{:S(2)}) collective-permute-start(bf16[320,2048]{1,0:T(8,128)(2,1)} %slice.249), channel_id=1, source_target_pairs={{8,0},{12,4},{0,8},{4,12},{24,16},{28,20},{16,24},{20,28},{9,1},{1... | collective-permute-start | bytes 3932168 | tf_op jit(solution)/shard_map/ppermute | solution.py:258
  75.2 77.8 %collective-permute-start.1 = (f16[960,640]{1,0:T(8,128)(2,1)}, f16[960,640]{1,0:T(8,128)(2,1)}, u32[]{:S(2)}, u32[]{:S(2)}) collective-permute-start(f16[960,640]{1,0:T(8,128)(2,1)} %reduce-precision_convert_fusion.1), channel_id=1, source_target_pairs={{0,1},{3,2},{4,5},{7,6},{8,9},{11,10},{12,13},{15,14},{16,17},{19,... | collective-permute-start | bytes 3686408 | tf_op jit(solution)/shard_map/ppermute | solution.py:250
  86.4 60.4 %collective-permute-start.6 = (f16[640,640]{0,1:T(8,128)(2,1)}, f16[640,640]{0,1:T(8,128)(2,1)S(1)}, u32[]{:S(2)}, u32[]{:S(2)}) collective-permute-start(f16[640,640]{0,1:T(8,128)(2,1)} %get-tuple-element.55), channel_id=1, source_target_pairs={{0,1},{3,2},{4,5},{7,6},{8,9},{11,10},{12,13},{15,14},{16,17},{19,... | collective-permute-start | bytes 2457608 | tf_op jit(solution)/shard_map/ppermute | solution.py:250
  94.4 55.7 %collective-permute-start.11 = (f16[640,640]{0,1:T(8,128)(2,1)}, f16[640,640]{0,1:T(8,128)(2,1)}, u32[]{:S(2)}, u32[]{:S(2)}) collective-permute-start(f16[640,640]{0,1:T(8,128)(2,1)} %get-tuple-element.57), channel_id=1, source_target_pairs={{0,1},{3,2},{4,5},{7,6},{8,9},{11,10},{12,13},{15,14},{16,17},{19,... | collective-permute-start | bytes 2457608 | tf_op jit(solution)/shard_map/ppermute | solution.py:250
  99.2 58.6 %collective-permute-start.16 = (bf16[320,2048]{1,0:T(8,128)(2,1)}, bf16[320,2048]{1,0:T(8,128)(2,1)}, u32[]{:S(2)}, u32[]{:S(2)}) collective-permute-start(bf16[320,2048]{1,0:T(8,128)(2,1)} %slice.250), channel_id=1, source_target_pairs={{16,0},{20,4},{28,8},{24,12},{4,16},{0,20},{8,24},{12,28},{17,1},{... | collective-permute-start | bytes 3932168 | tf_op jit(solution)/shard_map/ppermute | solution.py:258
  155.7 69.2 %collective-permute-start.2 = (f16[960,640]{1,0:T(8,128)(2,1)S(1)}, f16[960,640]{1,0:T(8,128)(2,1)S(1)}, u32[]{:S(2)}, u32[]{:S(2)}) collective-permute-start(f16[960,640]{1,0:T(8,128)(2,1)S(1)} %reduce-precision_convert_fusion), channel_id=1, source_target_pairs={{1,2},{2,1},{5,6},{6,5},{9,10},{10,9},{13,14},{14,13},{17,18},{18,... | collective-permute-start | bytes 3686408 | tf_op jit(solution)/shard_map/ppermute | solution.py:252
  178.4 44.8 %collective-permute-start.8 = (f16[640,640]{0,1:T(8,128)(2,1)S(1)}, f16[640,640]{0,1:T(8,128)(2,1)S(1)}, u32[]{:S(2)}, u32[]{:S(2)}) collective-permute-start(f16[640,640]{0,1:T(8,128)(2,1)S(1)} %fusion.5), channel_id=1, source_target_pairs={{1,0},{2,3},{5,4},{6,7},{9,8},{10,11},{13,12},{14,15},{17,16},{18,... | collective-permute-start | bytes 2457608 | tf_op jit(solution)/shard_map/ppermute | solution.py:254
  188.4 42.2 %collective-permute-start.18 = (f16[640,640]{0,1:T(8,128)(2,1)S(1)}, f16[640,640]{0,1:T(8,128)(2,1)S(1)}, u32[]{:S(2)}, u32[]{:S(2)}) collective-permute-start(f16[640,640]{0,1:T(8,128)(2,1)S(1)} %reduce-precision_convert_fusion.2), channel_id=1, source_target_pairs={{1,2},{2,1},{5,6},{6,5},{9,10},{10,9},{13,14},{14,13},{17,18},{18,... | collective-permute-start | bytes 2457608 | tf_op jit(solution)/shard_map/ppermute | solution.py:252
  287.5 113.3 %collective-permute-start.4 = (f16[960,640]{1,0:T(8,128)(2,1)S(1)}, f16[960,640]{1,0:T(8,128)(2,1)}, u32[]{:S(2)}, u32[]{:S(2)}) collective-permute-start(f16[960,640]{1,0:T(8,128)(2,1)S(1)} %get-tuple-element.14), channel_id=1, source_target_pairs={{0,4},{4,0},{8,12},{12,8},{16,20},{20,16},{24,28},{28,24},{1,5},{5... | collective-permute-start | bytes 3686408 | tf_op jit(solution)/shard_map/ppermute | solution.py:258
  294.5 88.4 %collective-permute-start.22 = (f16[640,640]{0,1:T(8,128)(2,1)}, f16[640,640]{0,1:T(8,128)(2,1)}, u32[]{:S(2)}, u32[]{:S(2)}) collective-permute-start(f16[640,640]{0,1:T(8,128)(2,1)} %get-tuple-element.18), channel_id=1, source_target_pairs={{0,8},{4,12},{8,4},{12,0},{16,24},{20,28},{24,20},{28,16},{1,9},{5... | collective-permute-start | bytes 2457608 | tf_op jit(solution)/shard_map/ppermute | solution.py:258
  294.6 100.4 %collective-permute-start.24 = (f16[640,640]{0,1:T(8,128)(2,1)}, f16[640,640]{0,1:T(8,128)(2,1)}, u32[]{:S(2)}, u32[]{:S(2)}) collective-permute-start(f16[640,640]{0,1:T(8,128)(2,1)} %get-tuple-element.18), channel_id=1, source_target_pairs={{0,4},{4,0},{8,12},{12,8},{16,20},{20,16},{24,28},{28,24},{1,5},{5... | collective-permute-start | bytes 2457608 | tf_op jit(solution)/shard_map/ppermute | solution.py:258
  295.7 119.6 %collective-permute-start.30 = (f16[960,640]{1,0:T(8,128)(2,1)S(1)}, f16[960,640]{1,0:T(8,128)(2,1)}, u32[]{:S(2)}, u32[]{:S(2)}) collective-permute-start(f16[960,640]{1,0:T(8,128)(2,1)S(1)} %get-tuple-element.14), channel_id=1, source_target_pairs={{0,16},{4,20},{8,24},{12,28},{16,4},{20,0},{24,12},{28,8},{1,17},{... | collective-permute-start | bytes 3686408 | tf_op jit(solution)/shard_map/ppermute | solution.py:258
  309.6 108.2 %collective-permute-start.28 = (f16[960,640]{1,0:T(8,128)(2,1)S(1)}, f16[960,640]{1,0:T(8,128)(2,1)}, u32[]{:S(2)}, u32[]{:S(2)}) collective-permute-start(f16[960,640]{1,0:T(8,128)(2,1)S(1)} %get-tuple-element.14), channel_id=1, source_target_pairs={{0,8},{4,12},{8,4},{12,0},{16,24},{20,28},{24,20},{28,16},{1,9},{5... | collective-permute-start | bytes 3686408 | tf_op jit(solution)/shard_map/ppermute | solution.py:258
  382.9 45.0 %collective-permute-start.21 = (f16[320,640]{0,1:T(8,128)(2,1)}, f16[320,640]{0,1:T(8,128)(2,1)}, u32[]{:S(2)}, u32[]{:S(2)}) collective-permute-start(f16[320,640]{0,1:T(8,128)(2,1)} %slice.251), channel_id=1, source_target_pairs={{8,0},{12,4},{0,8},{4,12},{24,16},{28,20},{16,24},{20,28},{9,1},{1... | collective-permute-start | bytes 1228808 | tf_op jit(solution)/shard_map/ppermute | solution.py:258
  400.9 59.7 %collective-permute-start.25 = (f16[640,640]{0,1:T(8,128)(2,1)}, f16[640,640]{0,1:T(8,128)(2,1)}, u32[]{:S(2)}, u32[]{:S(2)}) collective-permute-start(f16[640,640]{0,1:T(8,128)(2,1)} %collective-permute-done.22), channel_id=1, source_target_pairs={{0,4},{4,0},{8,12},{12,8},{16,20},{20,16},{24,28},{28,24},{1,5},{5... | collective-permute-start | bytes 2457608 | tf_op jit(solution)/shard_map/ppermute | solution.py:258
  415.3 58.1 %collective-permute-start.26 = (f16[640,640]{0,1:T(8,128)(2,1)}, f16[640,640]{0,1:T(8,128)(2,1)}, u32[]{:S(2)}, u32[]{:S(2)}) collective-permute-start(f16[640,640]{0,1:T(8,128)(2,1)} %collective-permute-done.20), channel_id=1, source_target_pairs={{0,4},{4,0},{8,12},{12,8},{16,20},{20,16},{24,28},{28,24},{1,5},{5... | collective-permute-start | bytes 2457608 | tf_op jit(solution)/shard_map/ppermute | solution.py:258
  417.8 40.7 %collective-permute-start.32 = (f16[480,640]{1,0:T(8,128)(2,1)}, f16[480,640]{1,0:T(8,128)(2,1)S(1)}, u32[]{:S(2)}, u32[]{:S(2)}) collective-permute-start(f16[480,640]{1,0:T(8,128)(2,1)} %slice.253), channel_id=1, source_target_pairs={{8,0},{12,4},{0,8},{4,12},{24,16},{28,20},{16,24},{20,28},{9,1},{1... | collective-permute-start | bytes 1843208 | tf_op jit(solution)/shard_map/ppermute | solution.py:258
  428.2 52.1 %collective-permute-start.29 = (f16[960,640]{1,0:T(8,128)(2,1)}, f16[960,640]{1,0:T(8,128)(2,1)}, u32[]{:S(2)}, u32[]{:S(2)}) collective-permute-start(f16[960,640]{1,0:T(8,128)(2,1)} %collective-permute-done.28), channel_id=1, source_target_pairs={{0,4},{4,0},{8,12},{12,8},{16,20},{20,16},{24,28},{28,24},{1,5},{5... | collective-permute-start | bytes 3686408 | tf_op jit(solution)/shard_map/ppermute | solution.py:258
  473.4 99.2 %collective-permute-start.49 = (bf16[640,2048]{1,0:T(8,128)(2,1)}, bf16[640,2048]{1,0:T(8,128)(2,1)}, u32[]{:S(2)}, u32[]{:S(2)}) collective-permute-start(bf16[640,2048]{1,0:T(8,128)(2,1)} %collective-permute-done.5.refs_4_), channel_id=1, source_target_pairs={{0,4},{4,0},{8,12},{12,8},{16,20},{20,16},{24,28},{28,24},{1,5},{5... | collective-permute-start | bytes 7864328 | tf_op jit(solution)/shard_map/ppermute | solution.py:258
  477.5 95.0 %collective-permute-start.50 = (bf16[640,2048]{1,0:T(8,128)(2,1)}, bf16[640,2048]{1,0:T(8,128)(2,1)}, u32[]{:S(2)}, u32[]{:S(2)}) collective-permute-start(bf16[640,2048]{1,0:T(8,128)(2,1)} %collective-permute-done.10.refs_6_), channel_id=1, source_target_pairs={{0,4},{4,0},{8,12},{12,8},{16,20},{20,16},{24,28},{28,24},{1,5},{5... | collective-permute-start | bytes 7864328 | tf_op jit(solution)/shard_map/ppermute | solution.py:258
  480.3 92.3 %collective-permute-start.51 = (bf16[640,2048]{1,0:T(8,128)(2,1)}, bf16[640,2048]{1,0:T(8,128)(2,1)S(1)}, u32[]{:S(2)}, u32[]{:S(2)}) collective-permute-start(bf16[640,2048]{1,0:T(8,128)(2,1)} %copy-done.17), channel_id=1, source_target_pairs={{0,4},{4,0},{8,12},{12,8},{16,20},{20,16},{24,28},{28,24},{1,5},{5... | collective-permute-start | bytes 7864328 | tf_op jit(solution)/shard_map/ppermute | solution.py:258
  (54 other events, 993.4 us)

commit v2 on v0

--- a/solution.py
+++ b/solution.py
@@ -2,15 +2,21 @@
 
 import jax
 import jax.numpy as jnp
+import numpy as np
 from jax import lax
+from jax.experimental import pallas as pl
+from jax.experimental.pallas import tpu as pltpu
 from jax.sharding import PartitionSpec as P
 
 coef_a = 3.4445
 coef_b = -4.775
 coef_c = 2.0315
 
-
-def local(iterate):
+SCALE_X = 32.0
+SCALE_G = SCALE_X * SCALE_X
+
+
+def plain(iterate):
     iter_b = iterate.astype(jnp.bfloat16)
     slab = lax.all_gather(iter_b, "row", axis=0, tiled=True)
     partial_value = lax.dot_general(
@@ -32,9 +38,521 @@
     return 0.2 * math.sqrt(columns_all) * (coef_a * iterate + product)
 
 
+def partner(r, d):
+    c, k = r // 2, r % 2
+    high = c & 1 if d == 1 else (c >> 1) & 1
+    return 2 * (c ^ d) + (k ^ high)
+
+
+def giver(r, d):
+    return next(q for q in range(8) if partner(q, d) == r)
+
+
+def on_chip(r, c):
+    return r // 2 == c
+
+
+FETCH = {d: [(partner(r, d), r) for r in range(8)] for d in (1, 2, 3)}
+GIVE = {d: [(q, partner(q, d)) for q in range(8)] for d in (1, 2, 3)}
+SIBLING = [(r, r ^ 1) for r in range(8)]
+
+
+def forward(via, held, wanted):
+    pairs = []
+    for r in range(8):
+        s = [s for s in range(8) if on_chip(s, (r // 2) ^ via) and held(s) == wanted(r)]
+        pairs.append((s[0], r))
+    return pairs
+
+
+FETCH_X = forward(1, lambda s: partner(s, 2), lambda r: partner(r, 3))
+FETCH_Y = forward(2, lambda s: partner(s, 1), lambda r: partner(r, 3))
+GIVE_X = forward(1, lambda s: giver(s, 2), lambda r: giver(r, 3))
+GIVE_Y = forward(2, lambda s: giver(s, 1), lambda r: giver(r, 3))
+
+
+def device_order(r):
+    order = [r, r ^ 1]
+    for d in (1, 2, 3):
+        order += [partner(r, d), partner(r, d) ^ 1]
+        assert order[2 * d + 1] == giver(r, d)
+    return order
+
+
+OWN = (0, 1, 2, 4, 6)
+EARLY = [("d", 0), ("d", 1), ("d", 2), ("d", 4), ("e", 0), ("e", 2), ("e", 4)]
+EARLY += [(1, k) for k in (0, 1, 2, 3)] + [(2, k) for k in (0, 1, 4, 5)]
+CROSS = [(1, k) for k in (4, 5, 6, 7)] + [(2, k) for k in (2, 3, 6, 7)]
+MIDDLE = [("d", 6)] + CROSS + [(3, k) for k in (2, 3, 4, 5)]
+THEIRS = [("e", 6)] + CROSS + [(3, k) for k in (0, 1, 6, 7)]
+OURS = [(3, k) for k in (0, 1, 6, 7)]
+FIELDS = 5
+
+
+def table(wanted, columns, keep):
+    out = []
+    for r in range(8):
+        order = device_order(r)
+        slot = {q: i for i, q in enumerate(order)}
+        goal = {k: columns.index(k) if k in columns else -1 for k in range(8)}
+        line = [r % 2] + [0] * (FIELDS - 1)
+        for kind, k in wanted:
+            q = order[k]
+            first = q % 2 == 0
+            if kind == "d":
+                i = j = k
+            elif kind == "e":
+                i, j = slot[q - q % 2], slot[q - q % 2 + 1]
+            else:
+                i, j = k, slot[partner(q, kind)]
+            line += [i, j, goal[i] if keep(kind, j) else -1, goal[j] if keep(kind, i) else -1, int(first)]
+        out.append(line)
+    return np.asarray(out, np.int32)
+
+
+def nt(a, b):
+    return lax.dot_general(a, b, (((1,), (1,)), ((), ())), preferred_element_type=jnp.float32)
+
+
+def own_kernel(me, x, sib, out):
+    size = x.shape[0]
+    half = size // 2
+    out[:size] = nt(x[...], x[...])
+
+    @pl.when(me[0] % 2 == 0)
+    def _():
+        out[size:] = nt(x[:half], sib[...])
+
+    @pl.when(me[0] % 2 == 1)
+    def _():
+        out[size:] = nt(sib[half:], x[...])
+
+
+def pairs_kernel(x, *refs):
+    halves, (out, peer) = refs[:-2], refs[-2:]
+    size = x.shape[0]
+    half = size // 2
+    for k in range(len(halves) // 2):
+        peer[:half], peer[half:] = halves[2 * k][...], halves[2 * k + 1][...]
+        out[k * size : (k + 1) * size] = nt(x[...], peer[...])
+
+
+def own_blocks(me, x, sib):
+    size, width = x.shape
+    vmem = pl.BlockSpec(memory_space=pltpu.VMEM)
+    return pl.pallas_call(
+        own_kernel,
+        in_specs=[pl.BlockSpec(memory_space=pltpu.SMEM), vmem, vmem],
+        out_specs=vmem,
+        out_shape=jax.ShapeDtypeStruct((size + size // 2, size), jnp.float32),
+        compiler_params=pltpu.CompilerParams(vmem_limit_bytes=40 * 2**20),
+        cost_estimate=pl.CostEstimate(
+            flops=3 * size * size * width, bytes_accessed=8 * size * width, transcendentals=0
+        ),
+    )(me, x, sib)
+
+
+def pair_blocks(x, *halves):
+    size, width = x.shape
+    n = len(halves) // 2
+    vmem = pl.BlockSpec(memory_space=pltpu.VMEM)
+    return pl.pallas_call(
+        pairs_kernel,
+        in_specs=[vmem] * (1 + len(halves)),
+        out_specs=vmem,
+        out_shape=jax.ShapeDtypeStruct((n * size, size), jnp.float32),
+        scratch_shapes=[pltpu.VMEM(x.shape, x.dtype)],
+        compiler_params=pltpu.CompilerParams(vmem_limit_bytes=40 * 2**20),
+        cost_estimate=pl.CostEstimate(
+            flops=2 * n * size * size * width, bytes_accessed=4 * n * size * width, transcendentals=0
+        ),
+    )(x, *halves)
+
+
+def square_kernel(*refs, wanted, names, columns, lead, pairs, givers, first, last):
+    me, table = refs[:2]
+    sources = 1 + max(k for k, _ in names.values())
+    rest = refs[2 + sources :]
+
+    def block(kind, k, n):
+        source, row = names[kind, k]
+        return refs[2 + source].at[pl.ds(row, n)]
+
+    width, items = len(columns), len(wanted)
+    if not first:
+        before, rest = rest[0], rest[1:]
+    if last:
+        grams, rest = rest[:width], rest[width:]
+        outs, (total, panel, slots, sems, done) = rest[:-5], rest[-5:]
+    else:
+        total, panel, slots, sems, done = rest
+    size = panel.shape[0]
+    half = size // 2
+    base = me[0] * (FIELDS * (items + 1))
+    field = lambda n, k: table[base + FIELDS * (n + 1) + k]
+    core = table[base]
+
+    def fetch_pair(k, straight, slot):
+        low, high = block("e", k, half), block("e", k + 1, half)
+        top, bottom = slots.at[slot, pl.ds(0, half)], slots.at[slot, pl.ds(half, half)]
+
+        @pl.when(straight)
+        def _():
+            pltpu.make_async_copy(low, top, sems.at[slot]).start()
+            pltpu.make_async_copy(high, bottom, sems.at[slot]).start()
+
+        @pl.when(jnp.logical_not(straight))
+        def _():
+            pltpu.make_async_copy(high, top, sems.at[slot]).start()
+            pltpu.make_async_copy(low, bottom, sems.at[slot]).start()
+
+    def fetch(ref, slot):
+        pltpu.make_async_copy(ref, slots.at[slot], sems.at[slot]).start()
+
+    def wait(slot):
+        pltpu.make_async_copy(slots.at[1 - slot], slots.at[slot], sems.at[slot]).wait()
+
+    at = lambda k: pl.ds(k * size, size)
+    straight = [pltpu.make_async_copy(block("d", 0, size), panel.at[:, at(0)], done.at[0])]
+    for d in range(1, pairs + 1):
+        straight.append(pltpu.make_async_copy(block(d, 0, size), panel.at[:, at(2 * d)], done.at[d]))
+    if not first:
+        straight.append(
+            pltpu.make_async_copy(before.at[:, pl.ds(lead * size, width * size)], total, done.at[4])
+        )
+    for copy in straight:
+        copy.start()
+    fetch_pair(0, core == 0, 0)
+    for d in range(1, givers + 1):
+        fetch(block(d, 2 * d + 1, size), d % 2)
+        wait((d - 1) % 2)
+        if d == 1:
+            @pl.when(core == 0)
+            def _():
+                panel[:, at(1)] = slots[0]
+
+            @pl.when(core == 1)
+            def _():
+                panel[:, at(1)] = slots[0].T
+        else:
+            panel[:, at(2 * d - 1)] = slots[(d - 1) % 2].T
+    wait(givers % 2)
+    panel[:, at(2 * givers + 1)] = slots[givers % 2].T
+
+    def start(n):
+        kind, k = wanted[n]
+        if kind == "e":
+            fetch_pair(k, field(n, 4) == 1, n % 2)
+        else:
+            fetch(block(kind, k, size), n % 2)
+
+    start(0)
+    if first:
+        total[...] = jnp.zeros_like(total)
+    for copy in straight:
+        copy.wait()
+
+    def body(n, carry):
+        for k in range(1, items):
+            @pl.when(n + 1 == k)
+            def _():
+                start(k)
+
+        slot = n % 2
+        wait(slot)
+        i, j, to_i, to_j = field(n, 0), field(n, 1), field(n, 2), field(n, 3)
+        spot = lambda k: pl.ds(pl.multiple_of(k * size, 128), size)
+
+        @pl.when(to_j >= 0)
+        def _():
+            total[:, spot(to_j)] += jnp.dot(
+                panel[:, spot(i)], slots[slot], preferred_element_type=jnp.float32
+            )
+
+        @pl.when(jnp.logical_and(to_i >= 0, i != j))
+        def _():
+            total[:, spot(to_i)] += nt(panel[:, spot(j)], slots[slot])
+
+        return carry
+
+    lax.fori_loop(0, items, body, 0)
+    if last:
+        for k in range(width):
+            gram = grams[k][...]
+            if columns[k] == 1:
+                gram = jnp.where(core == 0, gram, gram.T)
+            mixed = (coef_b / SCALE_G) * gram + (coef_c / SCALE_G**2) * total[:, at(k)]
+            outs[k][...] = mixed.astype(jnp.bfloat16)
+            if len(outs) > width:
+                outs[width + k][...] = mixed.T.astype(jnp.bfloat16)
+
+
+def square_update(
+    me, wanted, blocks, size, columns=OWN, pairs=3, givers=3, before=None, lead=0, grams=(),
+    turned=False, keep=lambda kind, slot: True,
+):
+    first, last, width, n = before is None, bool(grams), len(columns), len(wanted)
+    keys = [("d", 0), ("e", 0), ("e", 1)]
+    keys += [(d, 0) for d in range(1, pairs + 1)] + [(d, 2 * d + 1) for d in range(1, givers + 1)]
+    for kind, k in wanted:
+        keys += [("e", k), ("e", k + 1)] if kind == "e" else [(kind, k)]
+    arrays, names = [], {}
+    for key in keys:
+        array, row = blocks[key]
+        known = [k for k, a in enumerate(arrays) if a is array]
+        if not known:
+            arrays.append(array)
+        names[key] = (known[0] if known else len(arrays) - 1, row)
+    vmem, smem = pl.BlockSpec(memory_space=pltpu.VMEM), pl.BlockSpec(memory_space=pltpu.SMEM)
+    anywhere = pl.BlockSpec(memory_space=pl.ANY)
+    lines = jnp.asarray(table(wanted, columns, keep).reshape(-1))
+    scratch = [
+        pltpu.VMEM((size, (pairs + givers + 2) * size), jnp.bfloat16),
+        pltpu.VMEM((2, size, size), jnp.bfloat16),
+        pltpu.SemaphoreType.DMA((2,)),
+        pltpu.SemaphoreType.DMA((5,)),
+    ]
+    shape = jax.ShapeDtypeStruct((size, width * size), jnp.float32)
+    if last:
+        scratch = [pltpu.VMEM(shape.shape, jnp.float32)] + scratch
+        shape = [jax.ShapeDtypeStruct((size, size), jnp.bfloat16)] * (width * (2 if turned else 1))
+    return pl.pallas_call(
+        lambda *refs: square_kernel(
+            *refs, wanted=wanted, names=names, columns=columns, lead=lead, pairs=pairs, givers=givers,
+            first=first, last=last,
+        ),
+        in_specs=[smem, smem] + [anywhere] * (len(arrays) + (not first)) + [vmem] * len(grams),
+        out_specs=[vmem] * len(shape) if last else vmem,
+        out_shape=shape,
+        scratch_shapes=scratch,
+        compiler_params=pltpu.CompilerParams(vmem_limit_bytes=48 * 2**20),
+        cost_estimate=pl.CostEstimate(
+            flops=3 * n * size**3, bytes_accessed=2 * n * size * size + 10 * size * size * width,
+            transcendentals=0,
+        ),
+    )(me, lines, *arrays, *([] if first else [before]), *grams)
+
+
+def last_kernel(*refs, blocks, scale, first):
+    mixed, slab = refs[:blocks], refs[blocks : 2 * blocks]
+    so_far, out, rows, tall = refs[2 * blocks :]
+    size = mixed[0].shape[0]
+
+    @pl.when(pl.program_id(0) == 0)
+    def _():
+        for k in range(blocks):
+            rows[:, k * size : (k + 1) * size] = mixed[k][...]
+
+    for k in range(blocks):
+        tall[k * size : (k + 1) * size] = slab[k][...]
+    total = jnp.dot(rows[...], tall[...], preferred_element_type=jnp.float32)
+    start = (scale * coef_a) * so_far[...] if first else so_far[...]
+    out[...] = start + (scale / SCALE_X) * total
+
+
+def last_product(mixed, slab, so_far, scale, first):
+    size, width = so_far.shape
+    tile, n = 512, len(mixed)
+    column = lambda k: pl.BlockSpec((size, tile), lambda s: (k, s))
+    whole = pl.BlockSpec((size, size), lambda s: (0, 0), pipeline_mode=pl.Buffered(1))
+    return pl.pallas_call(
+        lambda *refs: last_kernel(*refs, blocks=n, scale=scale, first=first),
+        grid=(width // tile,),
+        in_specs=[whole] * n + [column(k) for _, k in slab] + [column(0)],
+        out_specs=column(0),
+        out_shape=jax.ShapeDtypeStruct(so_far.shape, jnp.float32),
+        scratch_shapes=[
+            pltpu.VMEM((size, n * size), jnp.bfloat16),
+            pltpu.VMEM((n * size, tile), jnp.bfloat16),
+        ],
+        compiler_params=pltpu.CompilerParams(vmem_limit_bytes=52 * 2**20),
+        cost_estimate=pl.CostEstimate(
+            flops=2 * n * size * size * width, bytes_accessed=2 * (n + 4) * size * width,
+            transcendentals=0,
+        ),
+    )(*mixed, *[t for t, _ in slab], so_far)
+
+
+def encode(x):
+    near = lax.reduce_precision(x, 5, 10)
+    goal = lax.reduce_precision(x, 8, 7)
+    same = lax.reduce_precision(near, 8, 7) == goal
+    return jnp.where(same, near, near + 0.25 * (goal - near)).astype(jnp.float16)
+
+
+INWARD, ACROSS, OUTWARD = [(0, 1), (3, 2)], [(1, 2), (2, 1)], [(1, 0), (2, 3)]
+
+
+def send(x, pairs):
+    return lax.ppermute(x, "row", pairs)
+
+
+def sums(part, inner, last=encode):
+    half = lambda t: t.astype(jnp.float16)
+    got = yield lax.ppermute(half(part), "col", INWARD)
+    pair = part + got.astype(jnp.float32)
+    got = yield lax.ppermute(half(pair), "col", ACROSS)
+    mine = last(pair + got.astype(jnp.float32))
+    got = yield lax.ppermute(mine, "col", OUTWARD)
+    yield jnp.where(inner, mine, got)
+
+
+def near(unit):
+    return send(unit, GIVE[1]), send(unit, GIVE[2])
+
+
+def far(one, two, cut):
+    return send(two[:cut], GIVE_X), send(one[cut:], GIVE_Y)
+
+
+def stage(*values):
+    return lax.optimization_barrier(values)
+
+
+def local(iterate):
+    size, width = iterate.shape
+    half = size // 2
+    me = lax.axis_index("row").astype(jnp.int32)
+    core = me % 2
+    plane = lax.axis_index("col")
+    inner = (plane == 1) | (plane == 2)
+    f32 = lambda t: t.astype(jnp.float32)
+    short = lambda t: lax.reduce_precision(f32(t), 8, 7).astype(jnp.bfloat16)
+
+    round_x = lambda t: (t * SCALE_X).astype(jnp.bfloat16)
+    x, top, bottom = round_x(iterate), round_x(iterate[:half]), round_x(iterate[half:])
+    place = me.reshape(1)
+    xf = f32(x)
+    squares = jnp.sum(xf * xf, axis=1)
+    eye = lax.broadcasted_iota(jnp.int32, (size, size), 0) == lax.broadcasted_iota(
+        jnp.int32, (size, size), 1
+    )
+
+    sib = send(x, SIBLING)
+    two_top, one_bottom = send(top, FETCH[2]), send(bottom, FETCH[1])
+    diag_got = lax.ppermute(squares, "col", INWARD)
+    de_sum = sums(
+        own_blocks(place, x, sib),
+        inner,
+        lambda t: encode(jnp.concatenate([jnp.where(eye, diag[:, None], t[:size]), t[size:]])),
+    )
+    de_got = next(de_sum)
+    two_top, one_bottom, de_got, diag_got, top, bottom = stage(
+        two_top, one_bottom, de_got, diag_got, top, bottom
+    )
+    one_top, two_bottom = send(top, FETCH[1]), send(bottom, FETCH[2])
+    diag_pair = squares + diag_got
+    diag_got = lax.ppermute(diag_pair, "col", ACROSS)
+    de_got = de_sum.send(de_got)
+    one_top, two_bottom, de_got, diag_got, two_top, one_bottom = stage(
+        one_top, two_bottom, de_got, diag_got, two_top, one_bottom
+    )
+    three_top, three_bottom = send(two_top, FETCH_X), send(one_bottom, FETCH_Y)
+    diag = diag_pair + diag_got
+    de_got = de_sum.send(de_got)
+    sum_12 = sums(pair_blocks(x, one_top, one_bottom, two_top, two_bottom), inner)
+    got_12 = next(sum_12)
+    diag_got = lax.ppermute(diag, "col", OUTWARD)
+    three_top, three_bottom, de_got, got_12, diag, diag_got = stage(
+        three_top, three_bottom, de_got, got_12, diag, diag_got
+    )
+    unit_de = de_sum.send(de_got)
+    de = short(unit_de)
+    de_one, de_two = near(de)
+    de_sib = send(de, SIBLING)
+    got_12 = sum_12.send(got_12)
+    sum_3 = sums(pair_blocks(x, three_top, three_bottom), inner)
+    got_3 = next(sum_3)
+    got_12, got_3, diag, de_one, de_two, de_sib = stage(
+        got_12, got_3, diag, de_one, de_two, de_sib
+    )
+    de_a, de_b = far(de_one, de_two, size)
+    de_near = send(jnp.concatenate([de_one, de_two]), SIBLING)
+    got_12 = sum_12.send(got_12)
+    got_3 = sum_3.send(got_3)
+    others = jnp.concatenate(
+        [one_top, one_bottom, two_top, two_bottom, three_top, three_bottom]
+    )
+    got_12, got_3, de_near, de_a, de_b, others = stage(
+        got_12, got_3, de_near, de_a, de_b, others
+    )
+    unit_12 = sum_12.send(got_12)
+    n12 = short(unit_12)
+    n12_one, n12_two = near(n12)
+    n12_sib = send(n12, SIBLING)
+    got_3 = sum_3.send(got_3)
+    de_far = send(jnp.concatenate([de_a, de_b]), SIBLING)
+    got_3, n12_one, n12_two, n12_sib, de_far, unit_de = stage(
+        got_3, n12_one, n12_two, n12_sib, de_far, unit_de
+    )
+    unit_3 = sum_3.send(got_3)
+    n3 = short(unit_3)
+    n3_one, n3_two = near(n3)
+    n12_a, n12_b = far(n12_one, n12_two, size)
+    n12_s = send(jnp.concatenate([n12_one, n12_two]), SIBLING)
+    rows = de.shape[0]
+    blocks = {}
+    for k, (t, at) in enumerate(
+        [(de, 0), (de_sib, 0), (de_near, 0), (de_one, 0), (de_near, rows), (de_two, 0), (de_far, 0)]
+    ):
+        blocks["d", k], blocks["e", k] = (t, at), (t, at + size)
+    blocks["d", 7], blocks["e", 7] = (de_a, 0), (de_b, 0)
+    rows = n12.shape[0]
+    for k, (t, at) in enumerate(
+        [(n12, 0), (n12_sib, 0), (n12_s, 0), (n12_one, 0), (n12_s, rows), (n12_two, 0)]
+    ):
+        blocks[1, k], blocks[2, k] = (t, at), (t, at + size)
+    total = square_update(place, EARLY, blocks, size, pairs=2, givers=2)
+    n3_one, n3_two, n12_a, n12_b, total, unit_de = stage(
+        n3_one, n3_two, n12_a, n12_b, total, unit_de
+    )
+    n3_a, n3_b = far(n3_one, n3_two, half)
+    n3_sib = send(n3, SIBLING)
+    n3_s = send(jnp.concatenate([n3_one, n3_two]), SIBLING)
+    n12_far = send(jnp.concatenate([n12_a, n12_b]), SIBLING)
+    blocks[1, 6], blocks[2, 6] = (n12_far, 0), (n12_far, size)
+    blocks[1, 7], blocks[2, 7] = (n12_a, 0), (n12_b, 0)
+    for k, t in enumerate([(n3, 0), (n3_sib, 0), (n3_s, 0), (n3_one, 0), (n3_s, size), (n3_two, 0)]):
+        blocks[3, k] = t
+    middle = square_update(
+        place, MIDDLE, blocks, size, OWN[2:], givers=2, before=total, lead=2,
+        keep=lambda kind, slot: slot != 7,
+    )
+    n3_a, n3_b, n3_sib, n3_s, n12_far, middle, others, unit_de = stage(
+        n3_a, n3_b, n3_sib, n3_s, n12_far, middle, others, unit_de
+    )
+    n3_ab = jnp.concatenate([n3_a, n3_b])
+    n3_far = send(n3_ab, SIBLING)
+    blocks[3, 6], blocks[3, 7] = (n3_far, 0), (n3_ab, 0)
+    mine, other = f32(unit_de[size:]), f32(send(unit_de[size:], SIBLING))
+    grams = [
+        jnp.where(eye, jnp.where(inner, diag, diag_got)[:, None], f32(unit_de[:size])),
+        jnp.where(core == 0, jnp.concatenate([mine, other]), jnp.concatenate([other, mine])),
+        f32(unit_12[:size]),
+        f32(unit_12[size:]),
+        f32(unit_3),
+    ]
+    others_s = send(others, SIBLING)
+    slab = [(x, 0), (sib, 0)]
+    for k in range(3):
+        slab += [(others, k), (others_s, k)]
+
+    *theirs, t1, t2, t3 = square_update(
+        place, THEIRS, blocks, size, OWN[2:], before=middle, grams=grams[2:], turned=True,
+        keep=lambda kind, slot: kind == 3 or slot == 7,
+    )
+    ours = square_update(place, OURS, blocks, size, OWN[:2], before=total, grams=grams[:2])
+    got = [send(t, GIVE[d]) for d, t in ((1, t1), (2, t2), (3, t3))]
+
+    scale = 0.2 * math.sqrt(width * lax.axis_size("col"))
+    most = last_product([*ours, *theirs], [slab[k] for k in OWN], iterate, scale, True)
+    return last_product(got, [slab[k] for k in (3, 5, 7)], most, scale, False)
+
+
 def solution(mesh):
+    suits = mesh.shape["row"] == 8 and mesh.shape["col"] == 4
     return jax.shard_map(
-        local,
+        local if suits else plain,
         mesh=mesh,
         in_specs=(P("row", "col"),),
         out_specs=P("row", "col"),

time: 726 us -> 425 us (0.59); the launches traced: 726 us -> 416 us
  waiting for transfers between devices: 646 us -> 197 us
  Pallas kernels: 0 us -> 124 us
  matrix products: 58.9 us -> 0 us
  starting transfers between devices: 0.35 us -> 50.2 us
  other arithmetic: 7.78 us -> 30.7 us
  local copies, waits for them, and re-layouts: 0.01 us -> 13.6 us
  between operations: 13.1 us -> 1.3 us
    all_gather x4 -> x0, waiting for transfers between devices: 425 us -> none  [the longest x1 120 us: local(): row_panel = lax.all_gather(gram_b, 'col', axis=1, tiled=True)]
    reduce_scatter x1 -> x0, waiting for transfers between devices: 220 us -> none  [local(): lax.psum_scatter(partial_value, 'col', scatter_dimension=1, tiled=True)]
    ppermute x0 -> x45, waiting for transfers between devices: none -> 197 us  [the longest x33 86.1 us: send(): return lax.ppermute(x, 'row', pairs)]
    pallas_call x0 -> x9, Pallas kernels: none -> 124 us  [the longest x4 84.5 us: square_update(): pl.pallas_call(lambda *refs: square_kernel(*refs, wanted=wanted, names=na...]
    dot_general x3 -> x0, matrix products: 58.9 us -> none  [the longest x1 22.1 us: local(): jnp.dot(lax.all_gather(mixed, 'col', axis=1, tiled=True), slab, preferred...]
    ppermute x0 -> x45, starting transfers between devices: none -> 50.2 us  [the longest x33 24.9 us: send(): return lax.ppermute(x, 'row', pairs)]
    convert_element_type x2 -> x16, other arithmetic: 7.78 us -> 23.3 us  [the longest x3 8.64 us: local(): short = lambda t: lax.reduce_precision(f32(t), 8, 7).astype(jnp.bfloat16)]
    unnamed x2 -> x104, local copies, waits for them, and re-layouts: 0.01 us -> 11.8 us
  transfers between devices with their start and end apart: 5 -> 45, of which waited for: 5 -> 21; matrix products, arithmetic and copies ran while one was open for 0% -> 7% of each run, Pallas kernels for 0% -> 27%
where the time goes in v2:
time: 425 us; the launch traced here: 416 us
  waiting for transfers between devices  197 us (46%)
  Pallas kernels  124 us (29%)
  starting transfers between devices  50.2 us (12%)
  other arithmetic  30.7 us (7%)
  local copies, waits for them, and re-layouts  13.6 us (3%)
    ppermute x33, waiting for transfers between devices, send(): return lax.ppermute(x, 'row', pairs)  86.1 us
    pallas_call x4, Pallas kernels, square_update(): pl.pallas_call(lambda *refs: square_kernel(*refs, wanted=wanted, names=na...  84.5 us
    ppermute x3, waiting for transfers between devices, sums(): got = (yield lax.ppermute(mine, 'col', OUTWARD))  38.3 us
    ppermute x1, waiting for transfers between devices, local(): diag_got = lax.ppermute(diag, 'col', OUTWARD)  28.5 us
    pallas_call x2, Pallas kernels, last_product(): pl.pallas_call(lambda *refs: last_kernel(*refs, blocks=n, scale=scale, fi...  25.8 us
    ppermute x33, starting transfers between devices, send(): return lax.ppermute(x, 'row', pairs)  24.9 us
    ppermute x1, waiting for transfers between devices, local(): diag_got = lax.ppermute(squares, 'col', INWARD)  24.8 us
    ppermute x3, waiting for transfers between devices, sums(): got = (yield lax.ppermute(half(part), 'col', INWARD))  19.2 us
  transfers between devices with their start and end apart: 45, of which 21 were waited for; matrix products, arithmetic and copies ran while one was open for 7% of the time, Pallas kernels for 27%

profile of v2, /device:TPU:0, one launch (start us, length us, event | category | flops | bytes accessed | tf_op | source)
XLA Modules:
  0.0 416.2 jit_solution(1369736970022623900)
XLA Ops:
  10.4 5.2 %shard_map.55 = f32[960,640]{1,0:T(8,128)S(1)} custom-call(s32[1]{0:T(128)} %bitcast.me.refs_0_, bf16[640,2048]{1,0:T(8,128)(2,1)S(1)} %get-tuple-element.122.x.refs_5_, bf16[640,2048]{1,0:T(8,128)(2,1)} %collective-permute-done.2.sib.refs_6_), custom_call_target="tpu_custom_call" | custom-call | flops 2516582400 | bytes 10485760 | tf_op jit(solution)/shard_map/pallas_call | solution.py:143
  20.8 24.8 %collective-permute-done.4 = f32[640]{0:T(1024)S(1)} collective-permute-done((f32[640]{0:T(1024)S(1)}, f32[640]{0:T(1024)S(1)}, u32[]{:S(2)}, u32[]{:S(2)}) %collective-permute-start.4) | collective-permute-done | bytes 2592 | tf_op jit(solution)/shard_map/ppermute | solution.py:433
  49.9 25.6 %collective-permute-done.5.refs_0_ = bf16[320,2048]{1,0:T(8,128)(2,1)S(1)} collective-permute-done((bf16[320,2048]{1,0:T(8,128)(2,1)}, bf16[320,2048]{1,0:T(8,128)(2,1)S(1)}, u32[]{:S(2)}, u32[]{:S(2)}) %collective-permute-start.5) | collective-permute-done | bytes 1310752 | tf_op jit(solution)/shard_map/ppermute | solution.py:387
  79.5 6.0 %shard_map.56 = f32[1280,640]{1,0:T(8,128)S(1)} custom-call(bf16[640,2048]{1,0:T(8,128)(2,1)S(1)} %copy-done.1, bf16[320,2048]{1,0:T(8,128)(2,1)S(1)} %collective-permute-done.5.refs_0_, bf16[320,2048]{1,0:T(8,128)(2,1)} %collective-permute-done.1.refs_1_, bf16[320,2048]{1,0:T(8,128)(2,1)} %collective-permute-done.refs_2_, ...), custom_call_target="tpu_custom_call" | custom-call | flops 3355443200 | bytes 10485760 | tf_op jit(solution)/shard_map/pallas_call | solution.py:159
  85.7 4.9 %collective-permute-start.12 = (f16[1280,640]{1,0:T(8,128)(2,1)S(1)}, f16[1280,640]{1,0:T(8,128)(2,1)S(1)}, u32[]{:S(2)}, u32[]{:S(2)}) collective-permute-start(f16[1280,640]{1,0:T(8,128)(2,1)S(1)} %convert_element_type.100), channel_id=1, source_target_pairs={{0,1},{3,2},{4,5},{7,6},{8,9},{11,10},{12,13},{15,14},{16,17},{19,... | collective-permute-start | bytes 4915208 | tf_op jit(solution)/shard_map/ppermute | solution.py:392
  96.4 28.5 %collective-permute-done.13 = f32[640]{0:T(1024)S(1)} collective-permute-done((f32[640]{0:T(1024)S(1)}, f32[640]{0:T(1024)S(1)}, u32[]{:S(2)}, u32[]{:S(2)}) %collective-permute-start.13) | collective-permute-done | bytes 2592 | tf_op jit(solution)/shard_map/ppermute | solution.py:455
  129.6 5.2 %reduce-precision_convert_fusion.1 = (bf16[960,640]{1,0:T(8,128)(2,1)S(1)}, f16[960,640]{1,0:T(8,128)(2,1)}) fusion(f16[960,640]{1,0:T(8,128)(2,1)} %copy-done.42, pred[]{:T(512)S(6)} %or.3, f32[320,640]{1,0:T(8,128)} %copy-done.36, f32[640,640]{1,0:T(8,128)} %copy-done.33), kind=kLoop, calls=%fused_computation.15 | loop fusion | flops 8601600 | bytes 6144001 | tf_op jit(solution)/shard_map/convert_element_type | solution.py:420
  139.0 5.9 %collective-permute-start.15 = (f16[640,640]{1,0:T(8,128)(2,1)S(1)}, f16[640,640]{1,0:T(8,128)(2,1)S(1)}, u32[]{:S(2)}, u32[]{:S(2)}) collective-permute-start(f16[640,640]{1,0:T(8,128)(2,1)S(1)} %convert_element_type.105), channel_id=1, source_target_pairs={{0,1},{3,2},{4,5},{7,6},{8,9},{11,10},{12,13},{15,14},{16,17},{19,... | collective-permute-start | bytes 2457608 | tf_op jit(solution)/shard_map/ppermute | solution.py:392
  144.9 18.1 %collective-permute-done.15 = f16[640,640]{1,0:T(8,128)(2,1)S(1)} collective-permute-done((f16[640,640]{1,0:T(8,128)(2,1)S(1)}, f16[640,640]{1,0:T(8,128)(2,1)S(1)}, u32[]{:S(2)}, u32[]{:S(2)}) %collective-permute-start.15) | collective-permute-done | bytes 819232 | tf_op jit(solution)/shard_map/ppermute | solution.py:392
  165.5 4.5 %fusion = f16[1280,640]{1,0:T(8,128)(2,1)S(1)} fusion(f16[1280,640]{1,0:T(8,128)(2,1)} %collective-permute-done.14, f32[1280,640]{1,0:T(8,128)S(1)} %shard_map.56, f16[1280,640]{1,0:T(8,128)(2,1)S(1)} %copy-done.40), kind=kLoop, calls=%fused_computation.4 | loop fusion | flops 10649600 | bytes 8192000 | tf_op jit(solution)/shard_map/convert_element_type | solution.py:380
  177.1 10.6 %collective-permute-done.23.refs_10_ = bf16[320,640]{1,0:T(8,128)(2,1)S(1)} collective-permute-done((bf16[320,640]{1,0:T(8,128)(2,1)S(1)}, bf16[320,640]{1,0:T(8,128)(2,1)S(1)}, u32[]{:S(2)}, u32[]{:S(2)}) %collective-permute-start.23) | collective-permute-done | bytes 409632 | tf_op jit(solution)/shard_map/ppermute | solution.py:387
  187.7 6.9 %collective-permute-done.22 = bf16[640,640]{1,0:T(8,128)(2,1)S(1)} collective-permute-done((bf16[640,640]{1,0:T(8,128)(2,1)S(1)}, bf16[640,640]{1,0:T(8,128)(2,1)S(1)}, u32[]{:S(2)}, u32[]{:S(2)}) %collective-permute-start.22) | collective-permute-done | bytes 819232 | tf_op jit(solution)/shard_map/ppermute | solution.py:387
  194.6 17.5 %collective-permute-done.19 = f16[1280,640]{1,0:T(8,128)(2,1)S(1)} collective-permute-done((f16[1280,640]{1,0:T(8,128)(2,1)S(1)}, f16[1280,640]{1,0:T(8,128)(2,1)S(1)}, u32[]{:S(2)}, u32[]{:S(2)}) %collective-permute-start.19) | collective-permute-done | bytes 1638432 | tf_op jit(solution)/shard_map/ppermute | solution.py:396
  218.9 20.8 %collective-permute-done.24 = f16[640,640]{1,0:T(8,128)(2,1)S(1)} collective-permute-done((f16[640,640]{1,0:T(8,128)(2,1)S(1)}, f16[640,640]{1,0:T(8,128)(2,1)S(1)}, u32[]{:S(2)}, u32[]{:S(2)}) %collective-permute-start.24) | collective-permute-done | bytes 819232 | tf_op jit(solution)/shard_map/ppermute | solution.py:396
  239.7 12.5 %collective-permute-done.25.refs_5_.refs_6_ = bf16[1280,640]{1,0:T(8,128)(2,1)S(1)} collective-permute-done((bf16[1280,640]{1,0:T(8,128)(2,1)S(1)}, bf16[1280,640]{1,0:T(8,128)(2,1)S(1)}, u32[]{:S(2)}, u32[]{:S(2)}) %collective-permute-start.25) | collective-permute-done | bytes 1638432 | tf_op jit(solution)/shard_map/ppermute | solution.py:387
  261.4 27.6 %shard_map.58.refs_16_.refs_11_ = f32[640,3200]{1,0:T(8,128)} custom-call(s32[1]{0:T(128)} %bitcast.me.refs_0_, s32[640]{0:T(1024)S(1)} %copy-done.30, bf16[960,640]{1,0:T(8,128)(2,1)S(1)} %get-tuple-element.119.refs_2_, bf16[960,640]{1,0:T(8,128)(2,1)S(1)} %collective-permute-done.18.refs_3_, bf16[1280,640]{1,0:T(8,128)(2,1)} %copy-done.37, ...), custom_call_target="tpu_custom_call" | custom-call | flops 11796480000 | bytes 32768000 | tf_op jit(solution)/shard_map/pallas_call | solution.py:319
  289.0 5.9 %collective-permute-done.31.refs_11_.refs_13_ = bf16[640,640]{1,0:T(8,128)(2,1)S(1)} collective-permute-done((bf16[640,640]{1,0:T(8,128)(2,1)S(1)}, bf16[640,640]{1,0:T(8,128)(2,1)S(1)}, u32[]{:S(2)}, u32[]{:S(2)}) %collective-permute-start.31) | collective-permute-done | bytes 819232 | tf_op jit(solution)/shard_map/ppermute | solution.py:387
  302.4 24.7 %shard_map.59.refs_17_ = f32[640,1920]{1,0:T(8,128)} custom-call(s32[1]{0:T(128)} %bitcast.me.refs_0_, s32[560]{0:T(1024)S(1)} %copy-done.29, bf16[960,640]{1,0:T(8,128)(2,1)S(1)} %get-tuple-element.119.refs_2_, bf16[960,640]{1,0:T(8,128)(2,1)} %copy-done.15, bf16[1280,640]{1,0:T(8,128)(2,1)} %copy-done.37, bf16[640,640]{1,0:T(8,128)(2,1)S(1)} %get-tuple-element.115.refs_5_, ...), custom_call_target="tpu_custom_call" | custom-call | flops 10223616000 | bytes 22937600 | tf_op jit(solution)/shard_map/pallas_call | solution.py:319
  332.9 8.4 %collective-permute-done.44 = f16[320,640]{1,0:T(8,128)(2,1)S(1)} collective-permute-done((f16[320,640]{1,0:T(8,128)(2,1)S(1)}, f16[320,640]{1,0:T(8,128)(2,1)S(1)}, u32[]{:S(2)}, u32[]{:S(2)}) %collective-permute-start.44) | collective-permute-done | bytes 409632 | tf_op jit(solution)/shard_map/ppermute | solution.py:387
  343.7 20.3 %shard_map.60 = (bf16[640,640]{1,0:T(8,128)(2,1)S(1)}, bf16[640,640]{1,0:T(8,128)(2,1)S(1)}, bf16[640,640]{1,0:T(8,128)(2,1)S(1)}, bf16[640,640]{1,0:T(8,128)(2,...) custom-call(s32[1]{0:T(128)} %bitcast.me.refs_0_, s32[560]{0:T(1024)S(1)} %copy-done.28, ...), custom_call_target="tpu_custom_call" | custom-call | flops 10223616000 | bytes 22937600 | tf_op jit(solution)/shard_map/pallas_call | solution.py:319
  370.2 11.9 %shard_map.61 = (bf16[640,640]{1,0:T(8,128)(2,1)S(1)}, bf16[640,640]{1,0:T(8,128)(2,1)S(1)}) custom-call(s32[1]{0:T(128)} %bitcast.me.refs_0_, s32[200]{0:T(256)S(1)} %copy-done.27, bf16[960,640]{1,0:T(8,128)(2,1)S(1)} %copy-done.8, bf16[960,640]{1,0:T(8,128)(2,1)} %copy-done.15, bf16[1280,640]{1,0:T(8,128)(2,1)} %copy-done.37, ...), custom_call_target="tpu_custom_call" | custom-call | flops 3145728000 | bytes 11468800 | tf_op jit(solution)/shard_map/pallas_call | solution.py:319
  382.1 15.0 %shard_map.62.refs_6_ = f32[640,2048]{1,0:T(8,128)} custom-call(bf16[640,640]{1,0:T(8,128)(2,1)S(1)} %get-tuple-element.110.refs_0_, bf16[640,640]{1,0:T(8,128)(2,1)S(1)} %get-tuple-element.111.refs_1_, bf16[640,640]{1,0:T(8,128)(2,1)} %copy-done.16, bf16[640,640]{1,0:T(8,128)(2,1)} %copy-done.17, bf16[640,640]{1,0:T(8,128)(2,1)} %copy-done.18, ...), custom_call_target="tpu_custom_call" | custom-call | flops 8388608000 | bytes 23592960 | tf_op jit(solution)/shard_map/pallas_call | solution.py:358
  397.1 6.9 %collective-permute-done.42.refs_2_ = bf16[640,640]{1,0:T(8,128)(2,1)S(1)} collective-permute-done((bf16[640,640]{1,0:T(8,128)(2,1)S(1)}, bf16[640,640]{1,0:T(8,128)(2,1)S(1)}, u32[]{:S(2)}, u32[]{:S(2)}) %collective-permute-start.42) | collective-permute-done | bytes 819232 | tf_op jit(solution)/shard_map/ppermute | solution.py:387
  404.9 10.9 %shard_map.63 = f32[640,2048]{1,0:T(8,128)} custom-call(bf16[640,640]{1,0:T(8,128)(2,1)S(1)} %collective-permute-done.40.refs_0_, bf16[640,640]{1,0:T(8,128)(2,1)S(1)} %collective-permute-done.41.refs_1_, bf16[640,640]{1,0:T(8,128)(2,1)} %copy-done.43, bf16[1920,2048]{1,0:T(8,128)(2,1)} %collective-permute-done.43.refs_3_.refs_4_.refs_5_, ...), custom_call_target="tpu_custom_call" | custom-call | flops 5033164800 | bytes 18350080 | tf_op jit(solution)/shard_map/pallas_call | solution.py:358
  (217 shorter events, 86.5 us)
Async XLA Ops:
  6.2 39.4 %collective-permute-start = (bf16[320,2048]{1,0:T(8,128)(2,1)}, bf16[320,2048]{1,0:T(8,128)(2,1)}, u32[]{:S(2)}, u32[]{:S(2)}) collective-permute-start(bf16[320,2048]{1,0:T(8,128)(2,1)} %get-tuple-element.61), channel_id=1, source_target_pairs={{16,0},{20,4},{24,8},{28,12},{4,16},{0,20},{12,24},{8,28},{17,1},{... | collective-permute-start | bytes 3932168 | tf_op jit(solution)/shard_map/ppermute | solution.py:387
  8.6 37.0 %collective-permute-start.1 = (bf16[320,2048]{1,0:T(8,128)(2,1)}, bf16[320,2048]{1,0:T(8,128)(2,1)}, u32[]{:S(2)}, u32[]{:S(2)}) collective-permute-start(bf16[320,2048]{1,0:T(8,128)(2,1)} %get-tuple-element.62), channel_id=1, source_target_pairs={{8,0},{12,4},{4,8},{0,12},{24,16},{28,20},{20,24},{16,28},{9,1},{1... | collective-permute-start | bytes 3932168 | tf_op jit(solution)/shard_map/ppermute | solution.py:387
  45.6 29.9 %collective-permute-start.5 = (bf16[320,2048]{1,0:T(8,128)(2,1)}, bf16[320,2048]{1,0:T(8,128)(2,1)S(1)}, u32[]{:S(2)}, u32[]{:S(2)}) collective-permute-start(bf16[320,2048]{1,0:T(8,128)(2,1)} %get-tuple-element.61), channel_id=1, source_target_pairs={{8,0},{12,4},{4,8},{0,12},{24,16},{28,20},{20,24},{16,28},{9,1},{1... | collective-permute-start | bytes 3932168 | tf_op jit(solution)/shard_map/ppermute | solution.py:387
  45.8 31.6 %collective-permute-start.6 = (bf16[320,2048]{1,0:T(8,128)(2,1)}, bf16[320,2048]{1,0:T(8,128)(2,1)S(1)}, u32[]{:S(2)}, u32[]{:S(2)}) collective-permute-start(bf16[320,2048]{1,0:T(8,128)(2,1)} %get-tuple-element.62), channel_id=1, source_target_pairs={{16,0},{20,4},{24,8},{28,12},{4,16},{0,20},{12,24},{8,28},{17,1},{... | collective-permute-start | bytes 3932168 | tf_op jit(solution)/shard_map/ppermute | solution.py:387
  77.4 47.4 %collective-permute-start.10 = (bf16[320,2048]{1,0:T(8,128)(2,1)}, bf16[320,2048]{1,0:T(8,128)(2,1)S(1)}, u32[]{:S(2)}, u32[]{:S(2)}) collective-permute-start(bf16[320,2048]{1,0:T(8,128)(2,1)} %collective-permute-done.1.refs_1_), channel_id=1, source_target_pairs={{16,0},{20,4},{28,8},{24,12},{4,16},{0,20},{8,24},{12,28},{17,1},{... | collective-permute-start | bytes 3932168 | tf_op jit(solution)/shard_map/ppermute | solution.py:387
  78.0 46.8 %collective-permute-start.9 = (bf16[320,2048]{1,0:T(8,128)(2,1)}, bf16[320,2048]{1,0:T(8,128)(2,1)S(1)}, u32[]{:S(2)}, u32[]{:S(2)}) collective-permute-start(bf16[320,2048]{1,0:T(8,128)(2,1)} %collective-permute-done.refs_2_), channel_id=1, source_target_pairs={{8,0},{12,4},{0,8},{4,12},{24,16},{28,20},{16,24},{20,28},{9,1},{1... | collective-permute-start | bytes 3932168 | tf_op jit(solution)/shard_map/ppermute | solution.py:387
  85.7 40.3 %collective-permute-start.12 = (f16[1280,640]{1,0:T(8,128)(2,1)S(1)}, f16[1280,640]{1,0:T(8,128)(2,1)S(1)}, u32[]{:S(2)}, u32[]{:S(2)}) collective-permute-start(f16[1280,640]{1,0:T(8,128)(2,1)S(1)} %convert_element_type.100), channel_id=1, source_target_pairs={{0,1},{3,2},{4,5},{7,6},{8,9},{11,10},{12,13},{15,14},{16,17},{19,... | collective-permute-start | bytes 4915208 | tf_op jit(solution)/shard_map/ppermute | solution.py:392
  93.8 31.1 %collective-permute-start.11 = (f16[960,640]{1,0:T(8,128)(2,1)S(1)}, f16[960,640]{1,0:T(8,128)(2,1)S(1)}, u32[]{:S(2)}, u32[]{:S(2)}) collective-permute-start(f16[960,640]{1,0:T(8,128)(2,1)S(1)} %fusion.1), channel_id=1, source_target_pairs={{1,0},{2,3},{5,4},{6,7},{9,8},{10,11},{13,12},{14,15},{17,16},{18,... | collective-permute-start | bytes 3686408 | tf_op jit(solution)/shard_map/ppermute | solution.py:396
  127.8 37.4 %collective-permute-start.14 = (f16[1280,640]{1,0:T(8,128)(2,1)}, f16[1280,640]{1,0:T(8,128)(2,1)}, u32[]{:S(2)}, u32[]{:S(2)}) collective-permute-start(f16[1280,640]{1,0:T(8,128)(2,1)} %fusion.2), channel_id=1, source_target_pairs={{1,2},{2,1},{5,6},{6,5},{9,10},{10,9},{13,14},{14,13},{17,18},{18,... | collective-permute-start | bytes 4915208 | tf_op jit(solution)/shard_map/ppermute | solution.py:394
  165.4 46.7 %collective-permute-start.21 = (bf16[1920,640]{1,0:T(8,128)(2,1)S(1)}, bf16[1920,640]{1,0:T(8,128)(2,1)S(1)}, u32[]{:S(2)}, u32[]{:S(2)}) collective-permute-start(bf16[1920,640]{1,0:T(8,128)(2,1)S(1)} %pad_maximum_fusion.2), channel_id=1, source_target_pairs={{0,4},{4,0},{8,12},{12,8},{16,20},{20,16},{24,28},{28,24},{1,5},{5... | collective-permute-start | bytes 7372808 | tf_op jit(solution)/shard_map/ppermute | solution.py:387
  170.0 42.1 %collective-permute-start.19 = (f16[1280,640]{1,0:T(8,128)(2,1)S(1)}, f16[1280,640]{1,0:T(8,128)(2,1)S(1)}, u32[]{:S(2)}, u32[]{:S(2)}) collective-permute-start(f16[1280,640]{1,0:T(8,128)(2,1)S(1)} %fusion), channel_id=1, source_target_pairs={{1,0},{2,3},{5,4},{6,7},{9,8},{10,11},{13,12},{14,15},{17,16},{18,... | collective-permute-start | bytes 4915208 | tf_op jit(solution)/shard_map/ppermute | solution.py:396
  214.1 38.1 %collective-permute-start.25 = (bf16[1280,640]{1,0:T(8,128)(2,1)S(1)}, bf16[1280,640]{1,0:T(8,128)(2,1)S(1)}, u32[]{:S(2)}, u32[]{:S(2)}) collective-permute-start(bf16[1280,640]{1,0:T(8,128)(2,1)S(1)} %get-tuple-element.117.refs_4_), channel_id=1, source_target_pairs={{0,8},{4,12},{8,4},{12,0},{16,24},{20,28},{24,20},{28,16},{1,9},{5... | collective-permute-start | bytes 4915208 | tf_op jit(solution)/shard_map/ppermute | solution.py:387
  215.5 37.8 %collective-permute-start.26 = (bf16[1280,640]{1,0:T(8,128)(2,1)S(1)}, bf16[1280,640]{1,0:T(8,128)(2,1)S(1)}, u32[]{:S(2)}, u32[]{:S(2)}) collective-permute-start(bf16[1280,640]{1,0:T(8,128)(2,1)S(1)} %get-tuple-element.117.refs_4_), channel_id=1, source_target_pairs={{0,16},{4,20},{8,24},{12,28},{16,4},{20,0},{24,12},{28,8},{1,17},{... | collective-permute-start | bytes 4915208 | tf_op jit(solution)/shard_map/ppermute | solution.py:387
  215.5 37.8 %collective-permute-start.27 = (bf16[1280,640]{1,0:T(8,128)(2,1)S(1)}, bf16[1280,640]{1,0:T(8,128)(2,1)S(1)}, u32[]{:S(2)}, u32[]{:S(2)}) collective-permute-start(bf16[1280,640]{1,0:T(8,128)(2,1)S(1)} %get-tuple-element.117.refs_4_), channel_id=1, source_target_pairs={{0,4},{4,0},{8,12},{12,8},{16,20},{20,16},{24,28},{28,24},{1,5},{5... | collective-permute-start | bytes 4915208 | tf_op jit(solution)/shard_map/ppermute | solution.py:387
  256.8 32.2 %collective-permute-start.29 = (bf16[640,640]{1,0:T(8,128)(2,1)S(1)}, bf16[640,640]{1,0:T(8,128)(2,1)S(1)}, u32[]{:S(2)}, u32[]{:S(2)}) collective-permute-start(bf16[640,640]{1,0:T(8,128)(2,1)S(1)} %get-tuple-element.115.refs_5_), channel_id=1, source_target_pairs={{0,8},{4,12},{8,4},{12,0},{16,24},{20,28},{24,20},{28,16},{1,9},{5... | collective-permute-start | bytes 2457608 | tf_op jit(solution)/shard_map/ppermute | solution.py:387
  257.0 32.0 %collective-permute-start.30 = (bf16[640,640]{1,0:T(8,128)(2,1)S(1)}, bf16[640,640]{1,0:T(8,128)(2,1)S(1)}, u32[]{:S(2)}, u32[]{:S(2)}) collective-permute-start(bf16[640,640]{1,0:T(8,128)(2,1)S(1)} %get-tuple-element.115.refs_5_), channel_id=1, source_target_pairs={{0,16},{4,20},{8,24},{12,28},{16,4},{20,0},{24,12},{28,8},{1,17},{... | collective-permute-start | bytes 2457608 | tf_op jit(solution)/shard_map/ppermute | solution.py:387
  258.4 36.5 %collective-permute-start.31 = (bf16[640,640]{1,0:T(8,128)(2,1)S(1)}, bf16[640,640]{1,0:T(8,128)(2,1)S(1)}, u32[]{:S(2)}, u32[]{:S(2)}) collective-permute-start(bf16[640,640]{1,0:T(8,128)(2,1)S(1)} %slice.49), channel_id=1, source_target_pairs={{8,0},{12,4},{0,8},{4,12},{24,16},{28,20},{16,24},{20,28},{9,1},{1... | collective-permute-start | bytes 2457608 | tf_op jit(solution)/shard_map/ppermute | solution.py:387
  259.3 35.8 %collective-permute-start.32 = (bf16[640,640]{1,0:T(8,128)(2,1)S(1)}, bf16[640,640]{1,0:T(8,128)(2,1)S(1)}, u32[]{:S(2)}, u32[]{:S(2)}) collective-permute-start(bf16[640,640]{1,0:T(8,128)(2,1)S(1)} %slice.50), channel_id=1, source_target_pairs={{16,0},{20,4},{28,8},{24,12},{4,16},{0,20},{8,24},{12,28},{17,1},{... | collective-permute-start | bytes 2457608 | tf_op jit(solution)/shard_map/ppermute | solution.py:387
  296.0 31.0 %collective-permute-start.36 = (bf16[640,640]{1,0:T(8,128)(2,1)S(1)}, bf16[640,640]{1,0:T(8,128)(2,1)S(1)}, u32[]{:S(2)}, u32[]{:S(2)}) collective-permute-start(bf16[640,640]{1,0:T(8,128)(2,1)S(1)} %get-tuple-element.115.refs_5_), channel_id=1, source_target_pairs={{0,4},{4,0},{8,12},{12,8},{16,20},{20,16},{24,28},{28,24},{1,5},{5... | collective-permute-start | bytes 2457608 | tf_op jit(solution)/shard_map/ppermute | solution.py:387
  296.2 30.9 %collective-permute-start.34 = (bf16[320,640]{1,0:T(8,128)(2,1)S(1)}, bf16[320,640]{1,0:T(8,128)(2,1)S(1)}, u32[]{:S(2)}, u32[]{:S(2)}) collective-permute-start(bf16[320,640]{1,0:T(8,128)(2,1)S(1)} %slice.51), channel_id=1, source_target_pairs={{8,0},{12,4},{0,8},{4,12},{24,16},{28,20},{16,24},{20,28},{9,1},{1... | collective-permute-start | bytes 1228808 | tf_op jit(solution)/shard_map/ppermute | solution.py:387
  327.1 76.9 %collective-permute-start.43 = (bf16[1920,2048]{1,0:T(8,128)(2,1)}, bf16[1920,2048]{1,0:T(8,128)(2,1)}, u32[]{:S(2)}, u32[]{:S(2)}) collective-permute-start(bf16[1920,2048]{1,0:T(8,128)(2,1)} %copy-done.31), channel_id=1, source_target_pairs={{0,4},{4,0},{8,12},{12,8},{16,20},{20,16},{24,28},{28,24},{1,5},{5... | collective-permute-start | bytes 23592968 | tf_op jit(solution)/shard_map/ppermute | solution.py:387
  365.8 31.3 %collective-permute-start.40 = (bf16[640,640]{1,0:T(8,128)(2,1)S(1)}, bf16[640,640]{1,0:T(8,128)(2,1)S(1)}, u32[]{:S(2)}, u32[]{:S(2)}) collective-permute-start(bf16[640,640]{1,0:T(8,128)(2,1)S(1)} %get-tuple-element.103), channel_id=1, source_target_pairs={{0,8},{4,12},{8,4},{12,0},{16,24},{20,28},{24,20},{28,16},{1,9},{5... | collective-permute-start | bytes 2457608 | tf_op jit(solution)/shard_map/ppermute | solution.py:387
  365.8 31.3 %collective-permute-start.41 = (bf16[640,640]{1,0:T(8,128)(2,1)S(1)}, bf16[640,640]{1,0:T(8,128)(2,1)S(1)}, u32[]{:S(2)}, u32[]{:S(2)}) collective-permute-start(bf16[640,640]{1,0:T(8,128)(2,1)S(1)} %get-tuple-element.104), channel_id=1, source_target_pairs={{0,16},{4,20},{8,24},{12,28},{16,4},{20,0},{24,12},{28,8},{1,17},{... | collective-permute-start | bytes 2457608 | tf_op jit(solution)/shard_map/ppermute | solution.py:387
  366.7 37.3 %collective-permute-start.42 = (bf16[640,640]{1,0:T(8,128)(2,1)S(1)}, bf16[640,640]{1,0:T(8,128)(2,1)S(1)}, u32[]{:S(2)}, u32[]{:S(2)}) collective-permute-start(bf16[640,640]{1,0:T(8,128)(2,1)S(1)} %get-tuple-element.105), channel_id=1, source_target_pairs={{0,24},{4,28},{8,16},{12,20},{16,12},{20,8},{24,4},{28,0},{1,25},{... | collective-permute-start | bytes 2457608 | tf_op jit(solution)/shard_map/ppermute | solution.py:387
  (70 other events, 1023.4 us)
